TPU v7x, 256 devices: a whole 4x4x8 slice. The times are simulated.
256 devices in a mesh: dp: 16 (over z, core), expert: 16 (over y, x).
Axes of the slice: x: 4, y: 4, z: 8, core: 2. Of those that a mesh axis runs over, the one named last changes fastest.
Arguments:
- tokens: bfloat16 [32768, 2048], P(('dp', 'expert')), may hold values from -24 to 24
- out_grad: bfloat16 [32768, 2048], P(('dp', 'expert')), may hold values from -6 to 6
- gates: bfloat16 [32768, 4], P(('dp', 'expert')), may hold values from 0.099609375 to 1
- expert_ids: int32 [32768, 4], P(('dp', 'expert')), may hold values from 0 to 15, all different within a row; in each aligned block of 128 rows (0 to 127, 128 to 255, ...) at most 40 rows name the same one
- w_gate: bfloat16 [16, 2048, 768], P('expert'), may hold values from -0.125 to 0.125
- w_up: bfloat16 [16, 2048, 768], P('expert'), may hold values from -0.125 to 0.125
- w_down: bfloat16 [16, 768, 2048], P('expert'), may hold values from -0.21875 to 0.21875
Outputs:
- token_grad: bfloat16 [32768, 2048], P(('dp', 'expert'))
- gate_grad: bfloat16 [32768, 4], P(('dp', 'expert'))
- grad_gate: bfloat16 [16, 2048, 768], P('expert', 'dp')
- grad_up: bfloat16 [16, 2048, 768], P('expert', 'dp')
- grad_down: bfloat16 [16, 768, 2048], P('expert', 'dp')
Inputs may be any that keep to these rules, and one draw needn't show every extreme that they name: `expert_ids`: in each aligned block of 128 rows (one device's tokens) no expert is named by more than 40 rows, a bound that some block reaches; a row names 4 different experts.
All inputs are finite; a program needn't handle non-finite values.
Results may differ from a plain program's by a relative error of at most 0.023.
Values may be sent and summed in bfloat16 or wider, within the bound.
No kernel may reach another device: no remote copies, remote signals or barrier semaphores. Data moves between devices by JAX's collectives and lax.ppermute only.
A program may use at most 128 MiB of HBM per device.

v0:
```python
import jax
import jax.numpy as jnp
from jax import lax
from jax.sharding import PartitionSpec as P


def body(tokens, out_grad, gates, expert_ids, w_gate, w_up, w_down):
    n_peer = lax.axis_size("expert")
    tok_rows = tokens.shape[0]
    width = tokens.shape[1]
    top_count = expert_ids.shape[1]
    exp_local = w_gate.shape[0]
    expert_total = exp_local * n_peer
    capacity = min(tok_rows, 5 * tok_rows * top_count // (4 * expert_total))
    slot_total = tok_rows * top_count
    flat_ids = expert_ids.reshape(-1)
    onehot = (flat_ids[:, None] == jnp.arange(expert_total, dtype=jnp.int32)[None, :]).astype(
        jnp.int32
    )
    earlier = jnp.cumsum(onehot, axis=0) - onehot
    position = jnp.sum(earlier * onehot, axis=1)
    dest = flat_ids * capacity + position
    slot_range = jnp.arange(slot_total, dtype=jnp.int32)
    slot_token = (
        jnp.full((expert_total * capacity,), tok_rows, jnp.int32)
        .at[dest]
        .set(slot_range // top_count)
    )
    slot_pick = jnp.full((expert_total * capacity,), slot_total, jnp.int32).at[dest].set(slot_range)
    x_pad = jnp.concatenate([tokens, jnp.zeros((1, width), jnp.bfloat16)], axis=0)
    dy_pad = jnp.concatenate([out_grad, jnp.zeros((1, width), jnp.bfloat16)], axis=0)
    gate_pad = jnp.concatenate([gates.reshape(-1), jnp.zeros((1,), jnp.bfloat16)], axis=0)
    send_x = x_pad[slot_token].reshape(n_peer, exp_local * capacity, width)
    send_dy = dy_pad[slot_token].reshape(n_peer, exp_local * capacity, width)
    send_gate = gate_pad[slot_pick].reshape(n_peer, exp_local * capacity)
    recv_x, recv_dy, recv_gate = (
        lax.all_to_all(send_x, "expert", split_axis=0, concat_axis=0, tiled=True),
        lax.all_to_all(send_dy, "expert", split_axis=0, concat_axis=0, tiled=True),
        lax.all_to_all(send_gate, "expert", split_axis=0, concat_axis=0, tiled=True),
    )
    recv_x = recv_x.reshape(n_peer, exp_local, capacity, width)
    recv_dy = recv_dy.reshape(n_peer, exp_local, capacity, width)
    probs = recv_gate.reshape(n_peer, exp_local, capacity).astype(jnp.float32)
    pre_gate = jnp.einsum("pecd,edf->pecf", recv_x, w_gate, preferred_element_type=jnp.float32)
    pre_up = jnp.einsum("pecd,edf->pecf", recv_x, w_up, preferred_element_type=jnp.float32)
    sigmoid_g = jax.nn.sigmoid(pre_gate)
    activated = pre_gate * sigmoid_g
    hidden = activated * pre_up
    back_hidden = jnp.einsum("pecd,efd->pecf", recv_dy, w_down, preferred_element_type=jnp.float32)
    prob_grad = jnp.sum(back_hidden * hidden, axis=-1).astype(jnp.bfloat16)
    scaled_hidden = (probs[..., None] * hidden).astype(jnp.bfloat16)
    d_hidden = probs[..., None] * back_hidden
    d_gate = (d_hidden * pre_up * sigmoid_g * (1.0 + pre_gate * (1.0 - sigmoid_g))).astype(
        jnp.bfloat16
    )
    d_up = (d_hidden * activated).astype(jnp.bfloat16)
    pair_grad = (
        jnp.einsum("pecf,edf->pecd", d_gate, w_gate, preferred_element_type=jnp.float32)
        + jnp.einsum("pecf,edf->pecd", d_up, w_up, preferred_element_type=jnp.float32)
    ).astype(jnp.bfloat16)
    back_rows, back_prob = (
        lax.all_to_all(
            pair_grad.reshape(n_peer, exp_local * capacity, width),
            "expert",
            split_axis=0,
            concat_axis=0,
            tiled=True,
        ),
        lax.all_to_all(
            prob_grad.reshape(n_peer, exp_local * capacity),
            "expert",
            split_axis=0,
            concat_axis=0,
            tiled=True,
        ),
    )
    back_rows = back_rows.reshape(expert_total * capacity, width)
    back_prob = back_prob.reshape(expert_total * capacity)
    token_grad = (
        back_rows[dest]
        .reshape(tok_rows, top_count, width)
        .astype(jnp.float32)
        .sum(axis=1)
        .astype(jnp.bfloat16)
    )
    gate_grad = back_prob[dest].reshape(tok_rows, top_count)
    term_gate = jnp.einsum("pecd,pecf->edf", recv_x, d_gate, preferred_element_type=jnp.float32)
    term_up = jnp.einsum("pecd,pecf->edf", recv_x, d_up, preferred_element_type=jnp.float32)
    term_down = jnp.einsum(
        "pecf,pecd->efd", scaled_hidden, recv_dy, preferred_element_type=jnp.float32
    )
    sum_gate, sum_up, sum_down = (
        lax.psum_scatter(
            term_gate.astype(jnp.bfloat16), "dp", scatter_dimension=1, tiled=True
        ).astype(jnp.float32),
        lax.psum_scatter(
            term_up.astype(jnp.bfloat16), "dp", scatter_dimension=1, tiled=True
        ).astype(jnp.float32),
        lax.psum_scatter(
            term_down.astype(jnp.bfloat16), "dp", scatter_dimension=1, tiled=True
        ).astype(jnp.float32),
    )
    grad_gate = sum_gate.astype(jnp.bfloat16)
    grad_up = sum_up.astype(jnp.bfloat16)
    grad_down = sum_down.astype(jnp.bfloat16)
    return (token_grad, gate_grad, grad_gate, grad_up, grad_down)


def solution(mesh):
    in_specs = (
        P(("dp", "expert"), None),
        P(("dp", "expert"), None),
        P(("dp", "expert"), None),
        P(("dp", "expert"), None),
        P("expert", None, None),
        P("expert", None, None),
        P("expert", None, None),
    )
    out_specs = (
        P(("dp", "expert"), None),
        P(("dp", "expert"), None),
        P("expert", "dp", None),
        P("expert", "dp", None),
        P("expert", "dp", None),
    )
    return jax.shard_map(body, mesh=mesh, in_specs=in_specs, out_specs=out_specs, check_vma=False)
```

profile of v0, /device:TPU:2, one launch (start us, length us, event | category | flops | bytes accessed | tf_op | source)
XLA Modules:
  0.0 324.2 jit_solution(12677913771325435203)
XLA Ops:
  14.3 4.3 %gather_fusion = bf16[640]{0:T(1024)(128)(2,1)S(1)} fusion(bf16[513]{0:T(1024)(128)(2,1)S(1)} %pad_maximum_fusion, s32[1024]{0:T(1024)S(1)} %pad_clamp_fusion.2), kind=kCustom, calls=%fused_computation | custom fusion | bytes 5120 | tf_op jit(solution)/shard_map/gather | solution.py:35
  19.3 7.5 %all-to-all-start = ((bf16[16,1,40]{2,1,0:T(2,128)(2,1)}), bf16[16,1,40]{2,1,0:T(2,128)(2,1)S(1)}, u32[]{:S(2)}, u32[]{:S(2)}) async-start(bf16[16,1,40]{2,1,0:T(2,128)(2,1)} %all_to_all.25), calls=%async_computation | async-start | bytes 16384 | tf_op jit(solution)/shard_map/all_to_all | solution.py:39
  31.2 8.0 %gather_fusion.2 = bf16[640,2048]{1,0:T(8,128)(2,1)} fusion(bf16[129,2048]{1,0:T(8,128)(2,1)} %concatenate.11, s32[1024]{0:T(1024)S(1)} %pad_clamp_fusion.1), kind=kCustom, calls=%fused_computation.2 | custom fusion | bytes 5245440 | tf_op jit(solution)/shard_map/gather | solution.py:33
  39.3 7.2 %all-to-all-start.2 = ((bf16[16,40,2048]{2,1,0:T(8,128)(2,1)}), bf16[16,40,2048]{2,1,0:T(8,128)(2,1)}, u32[]{:S(2)}, u32[]{:S(2)}) async-start(bf16[16,40,2048]{2,1,0:T(8,128)(2,1)} %bitcast.149), calls=%async_computation.2 | async-start | bytes 5242880 | tf_op jit(solution)/shard_map/all_to_all | solution.py:37
  48.4 8.1 %gather_fusion.1 = bf16[640,2048]{1,0:T(8,128)(2,1)} fusion(bf16[129,2048]{1,0:T(8,128)(2,1)} %concatenate.10, s32[1024]{0:T(1024)S(1)} %pad_clamp_fusion.1), kind=kCustom, calls=%fused_computation.1 | custom fusion | bytes 5245440 | tf_op jit(solution)/shard_map/gather | solution.py:34
  56.5 22.7 %all-to-all-done.2 = bf16[16,40,2048]{2,1,0:T(8,128)(2,1)} async-done(((bf16[16,40,2048]{2,1,0:T(8,128)(2,1)}), bf16[16,40,2048]{2,1,0:T(8,128)(2,1)}, u32[]{:S(2)}, u32[]{:S(2)}) %all-to-all-start.2) | async-done | bytes 2621472 | tf_op jit(solution)/shard_map/all_to_all | solution.py:37
  79.2 9.6 %all-to-all-start.1 = ((bf16[16,40,2048]{2,1,0:T(8,128)(2,1)}), bf16[16,40,2048]{2,1,0:T(8,128)(2,1)}, u32[]{:S(2)}, u32[]{:S(2)}) async-start(bf16[16,40,2048]{2,1,0:T(8,128)(2,1)} %bitcast.148), calls=%async_computation.1 | async-start | bytes 5242880 | tf_op jit(solution)/shard_map/all_to_all | solution.py:38
  89.1 5.4 %fusion.2 = f32[16,40,768]{2,1,0:T(8,128)} fusion(bf16[16,40,2048]{2,1,0:T(8,128)(2,1)} %all-to-all-done.2, bf16[1,2048,768]{2,1,0:T(8,128)(2,1)S(1)} %copy-done), kind=kOutput, calls=%fused_computation.13 | convolution fusion | flops 2013265920 | bytes 7733248 | tf_op jit(solution)/shard_map/pecd,edf->pecf/dot_general | solution.py:44
  94.4 5.4 %fusion.5 = f32[16,40,768]{2,1,0:T(8,128)} fusion(bf16[16,40,2048]{2,1,0:T(8,128)(2,1)} %all-to-all-done.2, bf16[1,2048,768]{2,1,0:T(8,128)(2,1)S(1)} %copy-done.1), kind=kOutput, calls=%fused_computation.16 | convolution fusion | flops 2013265920 | bytes 7733248 | tf_op jit(solution)/shard_map/pecd,edf->pecf/dot_general | solution.py:45
  99.8 20.9 %all-to-all-done.1 = bf16[16,40,2048]{2,1,0:T(8,128)(2,1)} async-done(((bf16[16,40,2048]{2,1,0:T(8,128)(2,1)}), bf16[16,40,2048]{2,1,0:T(8,128)(2,1)}, u32[]{:S(2)}, u32[]{:S(2)}) %all-to-all-start.1) | async-done | bytes 2621472 | tf_op jit(solution)/shard_map/all_to_all | solution.py:38
  120.6 7.4 %fusion.11 = bf16[1,768,2048]{2,1,0:T(8,128)(2,1)} fusion(bf16[16,40,2048]{2,1,0:T(8,128)(2,1)} %all-to-all-done.1, f32[16,40]{1,0:T(8,128)S(1)} %bitcast.154, f32[16,40,768]{2,1,0:T(8,128)} %fusion.5, f32[16,40,768]{2,1,0:T(8,128)} %fusion.2), kind=kOutput, calls=%fused_computation.22 | convolution fusion | flops 2018279424 | bytes 9701888 | tf_op jit(solution)/shard_map/pecf,pecd->efd/dot_general | solution.py:89
  128.1 7.7 %fusion.15 = (bf16[16,40]{1,0:T(8,128)(2,1)S(1)}, bf16[16,1,40,768]{3,2,0,1:T(8,128)(2,1)S(1)}, bf16[16,40,768]{2,1,0:T(8,128)(2,1)}) fusion(f32[16,40,768]{2,1,0:T(8,128)} %fusion.5, f32[16,40,768]{2,1,0:T(8,128)} %fusion.2, f32[16,40]{1,0:T(8,128)S(1)} %bitcast.155, bf16[16,40,2048]{2,1,0:T(8,128)(2,1)} %all-to-all-done.1, bf16[1,768,2048]{2,1,0:T(8,128)(2,1)} %param.13), kind=kOutput, calls=%fused_computation.30 | convolution fusion | flops 2021621120 | bytes 11669248 | tf_op jit(solution)/shard_map/pecd,efd->pecf/dot_general | solution.py:49
  136.8 6.1 %fusion.9 = bf16[1,2048,768]{2,1,0:T(8,128)(2,1)} fusion(bf16[16,40,2048]{2,1,0:T(8,128)(2,1)} %all-to-all-done.2, bf16[16,1,40,768]{3,2,0,1:T(8,128)(2,1)S(1)} %get-tuple-element.21), kind=kOutput, calls=%fused_computation.20 | convolution fusion | flops 2014838784 | bytes 6750208 | tf_op jit(solution)/shard_map/pecd,pecf->edf/dot_general | solution.py:87
  143.2 6.4 %fusion.10 = bf16[1,2048,768]{2,1,0:T(8,128)(2,1)} fusion(bf16[16,40,2048]{2,1,0:T(8,128)(2,1)} %all-to-all-done.2, bf16[16,40,768]{2,1,0:T(8,128)(2,1)} %get-tuple-element.22), kind=kOutput, calls=%fused_computation.21 | convolution fusion | flops 2014838784 | bytes 6750208 | tf_op jit(solution)/shard_map/pecd,pecf->edf/dot_general | solution.py:88
  150.2 7.3 %all-to-all-start.4 = ((bf16[16,1,40]{2,1,0:T(2,128)(2,1)}), bf16[16,1,40]{2,1,0:T(2,128)(2,1)S(1)}, u32[]{:S(2)}, u32[]{:S(2)}) async-start(bf16[16,1,40]{2,1,0:T(2,128)(2,1)} %copy.30), calls=%async_computation.4 | async-start | bytes 16384 | tf_op jit(solution)/shard_map/all_to_all | solution.py:69
  157.5 3.6 %fusion = f32[16,40,2048]{2,1,0:T(8,128)S(1)} fusion(bf16[1,2048,768]{2,1,0:T(8,128)(2,1)S(1)} %copy-done, bf16[16,1,40,768]{3,2,0,1:T(8,128)(2,1)} %copy-done.4), kind=kOutput, calls=%fused_computation.11 | convolution fusion | flops 2013265920 | bytes 9371648 | tf_op jit(solution)/shard_map/pecf,edf->pecd/dot_general | solution.py:58
  161.1 3.9 %add_convert_fusion = bf16[16,40,2048]{2,1,0:T(8,128)(2,1)} fusion(f32[16,40,2048]{2,1,0:T(8,128)S(1)} %fusion, bf16[16,40,768]{2,1,0:T(8,128)(2,1)S(1)} %copy-done.3, bf16[1,2048,768]{2,1,0:T(8,128)(2,1)S(1)} %copy-done.2), kind=kOutput, calls=%fused_computation.10 | convolution fusion | flops 2015887360 | bytes 11993088 | tf_op jit(solution)/shard_map/pecf,edf->pecd/dot_general | solution.py:59
  164.9 7.3 %all-to-all-start.3 = ((bf16[16,40,2048]{2,1,0:T(8,128)(2,1)}), bf16[16,40,2048]{2,1,0:T(8,128)(2,1)}, u32[]{:S(2)}, u32[]{:S(2)}) async-start(bf16[16,40,2048]{2,1,0:T(8,128)(2,1)} %add_convert_fusion), calls=%async_computation.3 | async-start | bytes 5242880 | tf_op jit(solution)/shard_map/all_to_all | solution.py:62
  176.7 27.7 %all-to-all-done.3 = bf16[16,40,2048]{2,1,0:T(8,128)(2,1)} async-done(((bf16[16,40,2048]{2,1,0:T(8,128)(2,1)}), bf16[16,40,2048]{2,1,0:T(8,128)(2,1)}, u32[]{:S(2)}, u32[]{:S(2)}) %all-to-all-start.3) | async-done | bytes 2621472 | tf_op jit(solution)/shard_map/all_to_all | solution.py:62
  204.4 7.5 %gather_fusion.3 = bf16[512,2048]{1,0:T(8,128)(2,1)} fusion(bf16[640,2048]{1,0:T(8,128)(2,1)} %bitcast.25, s32[1024]{0:T(1024)S(1)} %pad_clamp_fusion), kind=kCustom, calls=%fused_computation.3 | custom fusion | bytes 4196352 | tf_op jit(solution)/shard_map/gather | solution.py:80
  211.9 4.1 %reshape.162 = bf16[128,4,2048]{2,1,0:T(4,128)(2,1)} reshape(bf16[512,2048]{1,0:T(8,128)(2,1)} %gather_fusion.3) | data formatting | bytes 4194304 | tf_op jit(solution)/shard_map/reshape | solution.py:81
  216.0 5.0 %reduce_sum.34 = bf16[128,2048]{1,0:T(8,128)(2,1)} reduce(bf16[128,4,2048]{2,1,0:T(4,128)(2,1)} %reshape.162, bf16[]{:T(256)} %constant.37.clone.1), dimensions={1}, to_apply=%region_5.6 | reduce | flops 786432 | bytes 2621442 | tf_op jit(solution)/shard_map/reduce_sum | solution.py:83
  221.0 34.0 %reduce-scatter.4.cloned.1.call-done = bf16[1,128,768]{2,1,0:T(8,128)(2,1)} async-done(((bf16[1,2048,768]{2,1,0:T(8,128)(2,1)}), bf16[1,128,768]{2,1,0:T(8,128)(2,1)}) %reduce-scatter.4.cloned.1.call-update) | async-done | bytes 196624 | tf_op jit(solution)/shard_map/reduce_scatter | solution.py:93
  255.0 62.6 %reduce-scatter.6.cloned.1.call-done = bf16[1,128,768]{2,1,0:T(8,128)(2,1)} async-done(((bf16[1,2048,768]{2,1,0:T(8,128)(2,1)}), bf16[1,128,768]{2,1,0:T(8,128)(2,1)}) %reduce-scatter.6.cloned.1.call-update) | async-done | bytes 196624 | tf_op jit(solution)/shard_map/reduce_scatter | solution.py:96
  (54 shorter events, 20.7 us)
Async XLA Ops:
  7.2 81.9 %copy-start = (bf16[1,2048,768]{2,1,0:T(8,128)(2,1)S(1)}, bf16[1,2048,768]{2,1,0:T(8,128)(2,1)}, u32[]{:S(2)}) copy-start(bf16[1,2048,768]{2,1,0:T(8,128)(2,1)} %param.11) | copy-start | bytes 9437188
  19.3 19.9 %all-to-all-start = ((bf16[16,1,40]{2,1,0:T(2,128)(2,1)}), bf16[16,1,40]{2,1,0:T(2,128)(2,1)S(1)}, u32[]{:S(2)}, u32[]{:S(2)}) async-start(bf16[16,1,40]{2,1,0:T(2,128)(2,1)} %all_to_all.25), calls=%async_computation | async-start | bytes 16384 | tf_op jit(solution)/shard_map/all_to_all | solution.py:39
  39.3 39.9 %all-to-all-start.2 = ((bf16[16,40,2048]{2,1,0:T(8,128)(2,1)}), bf16[16,40,2048]{2,1,0:T(8,128)(2,1)}, u32[]{:S(2)}, u32[]{:S(2)}) async-start(bf16[16,40,2048]{2,1,0:T(8,128)(2,1)} %bitcast.149), calls=%async_computation.2 | async-start | bytes 5242880 | tf_op jit(solution)/shard_map/all_to_all | solution.py:37
  79.2 41.5 %all-to-all-start.1 = ((bf16[16,40,2048]{2,1,0:T(8,128)(2,1)}), bf16[16,40,2048]{2,1,0:T(8,128)(2,1)}, u32[]{:S(2)}, u32[]{:S(2)}) async-start(bf16[16,40,2048]{2,1,0:T(8,128)(2,1)} %bitcast.148), calls=%async_computation.1 | async-start | bytes 5242880 | tf_op jit(solution)/shard_map/all_to_all | solution.py:38
  88.8 132.2 %reduce-scatter.8.cloned.1.call-start = ((), (), s32[]{:S(2)}) async-start(), calls=%async_computation.10 | async-start | bytes 3342336 | tf_op jit(solution)/shard_map/reduce_scatter | solution.py:99
  89.1 5.4 %copy-start.1 = (bf16[1,2048,768]{2,1,0:T(8,128)(2,1)S(1)}, bf16[1,2048,768]{2,1,0:T(8,128)(2,1)}, u32[]{:S(2)}) copy-start(bf16[1,2048,768]{2,1,0:T(8,128)(2,1)} %param.12) | copy-start | bytes 9437188
  128.1 126.9 %reduce-scatter.4.cloned.1.call-start = ((), (), s32[]{:S(2)}) async-start(), calls=%async_computation.8 | async-start | bytes 3342336 | tf_op jit(solution)/shard_map/reduce_scatter | solution.py:93
  135.8 1.0 copy-start.4
  142.9 174.7 %reduce-scatter.6.cloned.1.call-start = ((), (), s32[]{:S(2)}) async-start(), calls=%async_computation.9 | async-start | bytes 3342336 | tf_op jit(solution)/shard_map/reduce_scatter | solution.py:96
  150.2 14.8 %all-to-all-start.4 = ((bf16[16,1,40]{2,1,0:T(2,128)(2,1)}), bf16[16,1,40]{2,1,0:T(2,128)(2,1)S(1)}, u32[]{:S(2)}, u32[]{:S(2)}) async-start(bf16[16,1,40]{2,1,0:T(2,128)(2,1)} %copy.30), calls=%async_computation.4 | async-start | bytes 16384 | tf_op jit(solution)/shard_map/all_to_all | solution.py:69
  157.4 3.6 %copy-start.2 = (bf16[1,2048,768]{2,1,0:T(8,128)(2,1)S(1)}, bf16[1,2048,768]{2,1,0:T(8,128)(2,1)}, u32[]{:S(2)}) copy-start(bf16[1,2048,768]{2,1,0:T(8,128)(2,1)} %param.12) | copy-start | bytes 9437188
  157.4 3.6 %copy-start.3 = (bf16[16,40,768]{2,1,0:T(8,128)(2,1)S(1)}, bf16[16,40,768]{2,1,0:T(8,128)(2,1)}, u32[]{:S(2)}) copy-start(bf16[16,40,768]{2,1,0:T(8,128)(2,1)} %get-tuple-element.22) | copy-start | bytes 2949124
  164.9 39.5 %all-to-all-start.3 = ((bf16[16,40,2048]{2,1,0:T(8,128)(2,1)}), bf16[16,40,2048]{2,1,0:T(8,128)(2,1)}, u32[]{:S(2)}, u32[]{:S(2)}) async-start(bf16[16,40,2048]{2,1,0:T(8,128)(2,1)} %add_convert_fusion), calls=%async_computation.3 | async-start | bytes 5242880 | tf_op jit(solution)/shard_map/all_to_all | solution.py:62
Sparse Core Ops, SparseCore 0:
  128.2 63.6 reduce-scatter.7
  195.0 59.9 reduce-scatter.3
  258.2 59.4 reduce-scatter.5
where the time goes:
time: 325 us; the launch traced here: 324 us
  waiting for transfers between devices  168 us (52%)
  local copies, waits for them, and re-layouts  49.9 us (15%)
  matrix products  45.7 us (14%)
  starting transfers between devices  39.4 us (12%)
  between operations  13.9 us (4%)
  other arithmetic  7.22 us (2%)
    reduce_scatter x1, waiting for transfers between devices, body(): lax.psum_scatter(term_up.astype(jnp.bfloat16), 'dp', scatter_dimension=1,...  62.6 us
    reduce_scatter x1, waiting for transfers between devices, body(): lax.psum_scatter(term_gate.astype(jnp.bfloat16), 'dp', scatter_dimension=...  34 us
    all_to_all x1, waiting for transfers between devices, body(): lax.all_to_all(pair_grad.reshape(n_peer, exp_local * capacity, width), 'e...  27.7 us
    all_to_all x1, waiting for transfers between devices, body(): lax.all_to_all(send_x, 'expert', split_axis=0, concat_axis=0, tiled=True)  22.7 us
    all_to_all x1, waiting for transfers between devices, body(): lax.all_to_all(send_dy, 'expert', split_axis=0, concat_axis=0, tiled=True)  20.9 us
    all_to_all x1, starting transfers between devices, body(): lax.all_to_all(send_dy, 'expert', split_axis=0, concat_axis=0, tiled=True)  9.62 us
    gather x1, local copies, waits for them, and re-layouts, body(): send_dy = dy_pad[slot_token].reshape(n_peer, exp_local * capacity, width)  8.06 us
    gather x1, local copies, waits for them, and re-layouts, body(): send_x = x_pad[slot_token].reshape(n_peer, exp_local * capacity, width)  8.05 us
  transfers between devices with their start and end apart: 8, of which 5 were waited for; matrix products, arithmetic and copies ran while one was open for 25% of the time, Pallas kernels for 0%

commit v1 on v0

v1 whole, which is shorter than its diff:
```python
import jax
import jax.numpy as jnp
from jax import lax
from jax.experimental import pallas as pl
from jax.experimental.pallas import tpu as pltpu
from jax.sharding import PartitionSpec as P

F32 = jnp.float32
BF16 = jnp.bfloat16
N_TOK = 128
D = 2048
FF = 768
CAP = 40
N_EXP = 16
ROWS = N_EXP * CAP
N_Z = 8
EXTRA = 128
VMEM_LIMIT = 48 * 1024 * 1024


def params():
    return pltpu.CompilerParams(vmem_limit_bytes=VMEM_LIMIT)


def cost(flops, nbytes):
    return pl.CostEstimate(flops=int(flops), bytes_accessed=int(nbytes), transcendentals=0)


def dot(a, b, ca=1, cb=0):
    return lax.dot_general(a, b, (((ca,), (cb,)), ((), ())), preferred_element_type=F32)


def slot_matrix(ids_t, gates_t=None):
    expert = lax.broadcasted_iota(jnp.int32, (N_EXP, N_TOK), 0)
    member = jnp.zeros((N_EXP, N_TOK), F32)
    weight = jnp.zeros((N_EXP, N_TOK), F32)
    for k in range(4):
        hit = ids_t[k : k + 1, :] == expert
        member = jnp.where(hit, 1.0, member)
        if gates_t is not None:
            weight = jnp.where(hit, gates_t[k : k + 1, :].astype(F32), weight)
    row = lax.broadcasted_iota(jnp.int32, (N_TOK, N_TOK), 0)
    col = lax.broadcasted_iota(jnp.int32, (N_TOK, N_TOK), 1)
    before = jnp.where(row < col, 1.0, 0.0).astype(BF16)
    position = dot(member.astype(BF16), before)
    code = jnp.where(member > 0.0, position, -1.0)
    slot = lax.broadcasted_iota(jnp.int32, (CAP, N_TOK), 0).astype(F32)
    pieces = []
    for e in range(N_EXP):
        value = 1.0 if gates_t is None else weight[e : e + 1, :]
        pieces.append(jnp.where(code[e : e + 1, :] == slot, value, 0.0))
    return jnp.concatenate(pieces, axis=0).astype(BF16)


def dispatch_kernel(ids_ref, x_ref, out_ref, slots):
    @pl.when(pl.program_id(0) == 0)
    def _():
        slots[...] = slot_matrix(ids_ref[...])

    out_ref[...] = dot(slots[...], x_ref[...]).astype(BF16)


def dispatch_gated_kernel(ids_ref, gates_ref, x_ref, out_ref, slots):
    @pl.when(pl.program_id(0) == 0)
    def _():
        slots[...] = slot_matrix(ids_ref[...], gates_ref[...])

    out_ref[...] = dot(slots[...], x_ref[...]).astype(BF16)


def dispatch(x, ids_t, gates_t=None):
    width = 512
    small = [pl.BlockSpec((4, N_TOK), lambda n: (0, 0))]
    args = [ids_t]
    if gates_t is not None:
        small = small * 2
        args.append(gates_t)
    return pl.pallas_call(
        dispatch_kernel if gates_t is None else dispatch_gated_kernel,
        grid=(D // width,),
        in_specs=small + [pl.BlockSpec((N_TOK, width), lambda n: (0, n))],
        out_specs=pl.BlockSpec((ROWS, width), lambda n: (0, n)),
        out_shape=jax.ShapeDtypeStruct((ROWS, D), BF16),
        scratch_shapes=[pltpu.VMEM((ROWS, N_TOK), BF16)],
        compiler_params=params(),
        cost_estimate=cost(2 * ROWS * N_TOK * D, 2 * ROWS * D),
    )(*args, x)


def forward_kernel(x_ref, wg_ref, wu_ref, ht_ref, h_ref, f_ref, a_ref):
    x = x_ref[...]
    g = dot(x, wg_ref[0])
    u = dot(x, wu_ref[0])
    s = jax.nn.sigmoid(g)
    a = g * s
    h = a * u
    h_ref[...] = h
    ht_ref[...] = h.T.astype(BF16)
    a_ref[...] = a
    f_ref[...] = u * s * (1.0 + g * (1.0 - s))


def forward(x, wg, wu):
    width = 256
    full = jax.ShapeDtypeStruct((ROWS, FF), F32)
    out = pl.BlockSpec((ROWS, width), lambda n: (0, n))
    return pl.pallas_call(
        forward_kernel,
        grid=(FF // width,),
        in_specs=[
            pl.BlockSpec((ROWS, D), lambda n: (0, 0)),
            pl.BlockSpec((1, D, width), lambda n: (0, 0, n)),
            pl.BlockSpec((1, D, width), lambda n: (0, 0, n)),
        ],
        out_specs=[pl.BlockSpec((width, ROWS), lambda n: (n, 0)), out, out, out],
        out_shape=[jax.ShapeDtypeStruct((FF, ROWS), BF16), full, full, full],
        compiler_params=params(),
        cost_estimate=cost(4 * ROWS * D * FF, 16_000_000),
    )(x, wg, wu)


def split_kernel(x_ref, out_ref):
    for c in range(2):
        out_ref[c, 0] = x_ref[:, c * 128 : (c + 1) * 128].T


def split_transposed(x):
    return pl.pallas_call(
        split_kernel,
        grid=(N_Z,),
        in_specs=[pl.BlockSpec((ROWS, 256), lambda n: (0, n))],
        out_specs=pl.BlockSpec((2, 1, 128, ROWS), lambda n: (0, n, 0, 0)),
        out_shape=jax.ShapeDtypeStruct((2, N_Z, 128, ROWS), BF16),
        compiler_params=params(),
        cost_estimate=cost(0, 4 * ROWS * D),
    )(x)


def backward_kernel(me_ref, dy_ref, wd_ref, h_ref, f_ref, a_ref, dg_ref, du_ref, gg_ref, total):
    n = pl.program_id(0)
    b = dot(dy_ref[...], wd_ref[0], 1, 1)
    dg_ref[...] = (b * f_ref[...]).astype(BF16)
    du_ref[...] = (b * a_ref[...]).astype(BF16)
    part = jnp.sum(b * h_ref[...], axis=1, keepdims=True)
    part = jnp.broadcast_to(part, (ROWS, EXTRA))

    @pl.when(n == 0)
    def _():
        total[...] = part

    @pl.when(n > 0)
    def _():
        total[...] += part

    @pl.when(n == pl.num_programs(0) - 1)
    def _():
        value = total[...]
        high = value.astype(BF16).astype(F32)
        col = lax.broadcasted_iota(jnp.int32, (ROWS, EXTRA), 1)
        me = me_ref[0]
        low = jnp.where(col == me + N_EXP, value - high, 0.0)
        gg_ref[...] = jnp.where(col == me, high, low).astype(BF16)


def backward(me, dy, wd, h, f, a):
    width = 256
    part = pl.BlockSpec((ROWS, width), lambda n: (0, n))
    return pl.pallas_call(
        backward_kernel,
        grid=(FF // width,),
        in_specs=[
            pl.BlockSpec(memory_space=pltpu.SMEM),
            pl.BlockSpec((ROWS, D), lambda n: (0, 0)),
            pl.BlockSpec((1, width, D), lambda n: (0, n, 0)),
            part,
            part,
            part,
        ],
        out_specs=[part, part, pl.BlockSpec((ROWS, EXTRA), lambda n: (0, 0))],
        out_shape=[
            jax.ShapeDtypeStruct((ROWS, FF), BF16),
            jax.ShapeDtypeStruct((ROWS, FF), BF16),
            jax.ShapeDtypeStruct((ROWS, EXTRA), BF16),
        ],
        scratch_shapes=[pltpu.VMEM((ROWS, EXTRA), F32)],
        compiler_params=params(),
        cost_estimate=cost(2 * ROWS * D * FF, 14_000_000),
    )(me, dy, wd, h, f, a)


def pair_kernel(dg_ref, du_ref, wg_ref, wu_ref, gg_ref, out_ref):
    n = pl.program_id(0)
    width = wg_ref.shape[1]
    value = dot(dg_ref[...], wg_ref[0], 1, 1) + dot(du_ref[...], wu_ref[0], 1, 1)
    out_ref[:, pl.ds(pl.multiple_of(n * width, width), width)] = value.astype(BF16)

    @pl.when(n == 0)
    def _():
        out_ref[:, D:] = gg_ref[...]


def pair_grads(dg, du, wg, wu, gg):
    width = 512
    whole = pl.BlockSpec((ROWS, FF), lambda n: (0, 0))
    weight = pl.BlockSpec((1, width, FF), lambda n: (0, n, 0))
    return pl.pallas_call(
        pair_kernel,
        grid=(D // width,),
        in_specs=[whole, whole, weight, weight, pl.BlockSpec((ROWS, EXTRA), lambda n: (0, 0))],
        out_specs=pl.BlockSpec((ROWS, D + EXTRA), lambda n: (0, 0)),
        out_shape=jax.ShapeDtypeStruct((ROWS, D + EXTRA), BF16),
        compiler_params=params(),
        cost_estimate=cost(4 * ROWS * D * FF, 12_000_000),
    )(dg, du, wg, wu, gg)


def outer_kernel(at_ref, bt_ref, a_ref, b_ref, out_ref):
    value = dot(at_ref[...], a_ref[...]) + dot(bt_ref[...], b_ref[...])
    out_ref[...] = value.astype(BF16)


def outer_sum(own_t, other_t, own, other):
    m, n, width = own_t.shape[0], own.shape[1], 256
    left = pl.BlockSpec((m, ROWS), lambda j: (0, 0))
    right = pl.BlockSpec((ROWS, width), lambda j: (0, j))
    return pl.pallas_call(
        outer_kernel,
        grid=(n // width,),
        in_specs=[left, left, right, right],
        out_specs=pl.BlockSpec((m, width), lambda j: (0, j)),
        out_shape=jax.ShapeDtypeStruct((m, n), BF16),
        compiler_params=params(),
        cost_estimate=cost(4 * ROWS * m * n, 2 * (m * n + 2 * ROWS * (m + n))),
    )(own_t, other_t, own, other)


def combine_kernel(ids_ref, gates_ref, rows_ref, extra_ref, tok_ref, gate_ref, slots):
    @pl.when(pl.program_id(0) == 0)
    def _():
        matrix = slot_matrix(ids_ref[...])
        slots[...] = matrix
        by_expert = dot(extra_ref[...], matrix, 0, 0)
        value = by_expert[:N_EXP] + by_expert[N_EXP : 2 * N_EXP]
        expert = lax.broadcasted_iota(jnp.int32, (N_EXP, N_TOK), 0)
        for k in range(4):
            mine = jnp.where(ids_ref[k : k + 1, :] == expert, value, 0.0)
            total = jnp.sum(mine, axis=0, keepdims=True)
            gate = gates_ref[k : k + 1, :].astype(F32)
            gate_ref[k : k + 1, :] = total / gate

    tok_ref[...] = dot(slots[...], rows_ref[...], 0, 0).astype(BF16)


def combine(ids_t, gates_t, rows):
    width = 512
    small = pl.BlockSpec((4, N_TOK), lambda n: (0, 0))
    return pl.pallas_call(
        combine_kernel,
        grid=(D // width,),
        in_specs=[
            small,
            small,
            pl.BlockSpec((ROWS, width), lambda n: (0, n)),
            pl.BlockSpec((ROWS, EXTRA), lambda n: (0, D // EXTRA)),
        ],
        out_specs=[pl.BlockSpec((N_TOK, width), lambda n: (0, n)), small],
        out_shape=[
            jax.ShapeDtypeStruct((N_TOK, D), BF16),
            jax.ShapeDtypeStruct((4, N_TOK), F32),
        ],
        scratch_shapes=[pltpu.VMEM((ROWS, N_TOK), BF16)],
        compiler_params=params(),
        cost_estimate=cost(2 * ROWS * N_TOK * D, 2 * ROWS * D),
    )(ids_t, gates_t, rows, rows)


def exchange_experts(rows):
    width = rows.shape[1]
    moved = lax.all_to_all(
        rows.reshape(N_EXP, CAP, width), "expert", split_axis=0, concat_axis=0, tiled=True
    )
    return moved.reshape(ROWS, width)


def swap_cores(a):
    return lax.ppermute(a, "dp", [(i, i ^ 1) for i in range(2 * N_Z)])


def pick(a, index):
    return lax.dynamic_index_in_dim(a, index, 0, keepdims=False)


def ring_sum(chains, z, core):
    sign = 1 - 2 * core
    route = []
    for i in range(N_Z):
        route.append((2 * i, 2 * ((i + 1) % N_Z)))
        route.append((2 * i + 1, 2 * ((i - 1) % N_Z) + 1))
    held = [pick(g, lax.rem(z - sign + 2 * N_Z, N_Z)) for g in chains]
    for step in range(2, N_Z + 1):
        block = lax.rem(z - step * sign + 2 * N_Z, N_Z)
        came = [lax.ppermute(a, "dp", route) for a in held]
        held = [
            (c.astype(F32) + pick(g, block).astype(F32)).astype(BF16)
            for c, g in zip(came, chains, strict=True)
        ]
    return held


def body(tokens, out_grad, gates, expert_ids, w_gate, w_up, w_down):
    dp = lax.axis_index("dp")
    z, core = dp // 2, lax.rem(dp, 2)
    me = lax.axis_index("expert").astype(jnp.int32).reshape(1)
    ids_t, gates_t = expert_ids.T, gates.T

    x = exchange_experts(dispatch(tokens, ids_t))
    dy = exchange_experts(dispatch(out_grad, ids_t, gates_t))

    hidden_t, hidden, factor, active = forward(x, w_gate, w_up)
    x_split = split_transposed(x)
    x_own = pick(x_split, core).reshape(D // 2, ROWS)
    x_other = swap_cores(pick(x_split, 1 - core)).reshape(D // 2, ROWS)
    hidden_other_t = swap_cores(hidden_t)

    dy_own = lax.dynamic_slice_in_dim(dy, core * (D // 2), D // 2, axis=1)
    dy_other = swap_cores(lax.dynamic_slice_in_dim(dy, (1 - core) * (D // 2), D // 2, axis=1))
    d_gate, d_up, prob = backward(me, dy, w_down, hidden, factor, active)
    d_gate_other, d_up_other = swap_cores(d_gate), swap_cores(d_up)

    rows = exchange_experts(pair_grads(d_gate, d_up, w_gate, w_up, prob))

    part_down = outer_sum(hidden_t, hidden_other_t, dy_own, dy_other)
    part_gate = outer_sum(x_own, x_other, d_gate, d_gate_other)
    part_up = outer_sum(x_own, x_other, d_up, d_up_other)
    sum_down, sum_gate, sum_up = ring_sum(
        [
            part_down.reshape(N_Z, FF // N_Z, D // 2),
            part_gate.reshape(N_Z, D // (2 * N_Z), FF),
            part_up.reshape(N_Z, D // (2 * N_Z), FF),
        ],
        z,
        core,
    )
    halves = sum_down.reshape(2, FF // (2 * N_Z), D // 2)
    mine = pick(halves, core)
    theirs = swap_cores(pick(halves, 1 - core))
    low = jnp.where(core == 0, mine, theirs)
    high = jnp.where(core == 0, theirs, mine)
    grad_down = jnp.concatenate([low, high], axis=1)

    token_grad, gate_grad_t = combine(ids_t, gates_t, rows)
    gate_grad = gate_grad_t.astype(BF16).T
    return token_grad, gate_grad, sum_gate[None], sum_up[None], grad_down[None]


def solution(mesh):
    both = P(("dp", "expert"), None)
    weight = P("expert", None, None)
    grad = P("expert", "dp", None)
    return jax.shard_map(
        body,
        mesh=mesh,
        in_specs=(both, both, both, both, weight, weight, weight),
        out_specs=(both, both, grad, grad, grad),
        check_vma=False,
    )
```

time: 325 us -> 198 us (0.61)
  waiting for transfers between devices: 168 us -> 80.3 us
  matrix products: 45.7 us -> 0 us
  Pallas kernels: 0 us -> 45 us
  local copies, waits for them, and re-layouts: 49.9 us -> 16 us
  between operations: 13.9 us -> 0.98 us
  starting transfers between devices: 39.4 us -> 45.5 us
    reduce_scatter x3 -> x0, waiting for transfers between devices: 96.7 us -> none  [the longest x1 62.6 us: body(): lax.psum_scatter(term_up.astype(jnp.bfloat16), 'dp', scatter_dimension=1,...]
    dot_general x8 -> x0, matrix products: 45.7 us -> none  [the longest x1 7.67 us: body(): jnp.einsum('pecd,efd->pecf', recv_dy, w_down, preferred_element_type=jnp....]
    pallas_call x0 -> x10, Pallas kernels: none -> 45 us  [the longest x3 14.5 us: outer_sum(): pl.pallas_call(outer_kernel, grid=(n // width,), in_specs=[left, left, ri...]
    gather x5 -> x0, local copies, waits for them, and re-layouts: 31.4 us -> none  [the longest x1 8.06 us: body(): send_dy = dy_pad[slot_token].reshape(n_peer, exp_local * capacity, width)]
    ppermute x0 -> x27, waiting for transfers between devices: none -> 30.3 us  [the longest x21 30.3 us: ring_sum(): came = [lax.ppermute(a, 'dp', route) for a in held]]
    all_to_all x5 -> x3, waiting for transfers between devices: 71.3 us -> 50 us  [exchange_experts(): lax.all_to_all(rows.reshape(N_EXP, CAP, width), 'expert', split_axis=0, c...]
    ppermute x0 -> x27, starting transfers between devices: none -> 19.9 us  [the longest x21 18.8 us: ring_sum(): came = [lax.ppermute(a, 'dp', route) for a in held]]
    all_to_all x5 -> x3, starting transfers between devices: 38.9 us -> 25.6 us  [exchange_experts(): lax.all_to_all(rows.reshape(N_EXP, CAP, width), 'expert', split_axis=0, c...]
  transfers between devices with their start and end apart: 8 -> 30, of which waited for: 5 -> 19; matrix products, arithmetic and copies ran while one was open for 25% -> 6% of each run, Pallas kernels for 0% -> 22%
where the time goes in v1:
time: 198 us; the launch traced here: 196 us
  waiting for transfers between devices  80.3 us (41%)
  starting transfers between devices  45.5 us (23%)
  Pallas kernels  45 us (23%)
  local copies, waits for them, and re-layouts  16 us (8%)
  other arithmetic  7.94 us (4%)
    all_to_all x3, waiting for transfers between devices, exchange_experts(): lax.all_to_all(rows.reshape(N_EXP, CAP, width), 'expert', split_axis=0, c...  50 us
    ppermute x21, waiting for transfers between devices, ring_sum(): came = [lax.ppermute(a, 'dp', route) for a in held]  30.3 us
    all_to_all x3, starting transfers between devices, exchange_experts(): lax.all_to_all(rows.reshape(N_EXP, CAP, width), 'expert', split_axis=0, c...  25.6 us
    ppermute x21, starting transfers between devices, ring_sum(): came = [lax.ppermute(a, 'dp', route) for a in held]  18.8 us
    pallas_call x3, Pallas kernels, outer_sum(): pl.pallas_call(outer_kernel, grid=(n // width,), in_specs=[left, left, ri...  14.5 us
    unnamed x32, local copies, waits for them, and re-layouts  10.5 us
    pallas_call x1, Pallas kernels, forward(): pl.pallas_call(forward_kernel, grid=(FF // width,), in_specs=[pl.BlockSpe...  8.7 us
    pallas_call x1, Pallas kernels, pair_grads(): pl.pallas_call(pair_kernel, grid=(D // width,), in_specs=[whole, whole, w...  7.08 us
  transfers between devices with their start and end apart: 30, of which 19 were waited for; matrix products, arithmetic and copies ran while one was open for 6% of the time, Pallas kernels for 22%

profile of v1, /device:TPU:2, one launch (start us, length us, event | category | flops | bytes accessed | tf_op | source)
XLA Modules:
  0.0 195.7 jit_solution(9136078358082059579)
XLA Ops:
  5.5 7.6 %all-to-all-start.1 = ((bf16[16,40,2048]{2,1,0:T(8,128)(2,1)}), bf16[16,40,2048]{2,1,0:T(8,128)(2,1)S(1)}, u32[]{:S(2)}, u32[]{:S(2)}) async-start(bf16[16,40,2048]{2,1,0:T(8,128)(2,1)} %bitcast.104), calls=%async_computation.1 | async-start | bytes 5242880 | tf_op jit(solution)/shard_map/all_to_all | solution.py:279
  16.4 31.5 %all-to-all-done.1 = bf16[16,40,2048]{2,1,0:T(8,128)(2,1)S(1)} async-done(((bf16[16,40,2048]{2,1,0:T(8,128)(2,1)}), bf16[16,40,2048]{2,1,0:T(8,128)(2,1)S(1)}, u32[]{:S(2)}, u32[]{:S(2)}) %all-to-all-start.1) | async-done | bytes 2621472 | tf_op jit(solution)/shard_map/all_to_all | solution.py:279
  47.9 9.3 %all-to-all-start = ((bf16[16,40,2048]{2,1,0:T(8,128)(2,1)}), bf16[16,40,2048]{2,1,0:T(8,128)(2,1)}, u32[]{:S(2)}, u32[]{:S(2)}) async-start(bf16[16,40,2048]{2,1,0:T(8,128)(2,1)} %bitcast.103), calls=%async_computation | async-start | bytes 5242880 | tf_op jit(solution)/shard_map/all_to_all | solution.py:279
  60.9 8.7 %shard_map.112 = (bf16[768,640]{1,0:T(8,128)(2,1)}, f32[640,768]{1,0:T(8,128)S(1)}, f32[640,768]{1,0:T(8,128)S(1)}, f32[640,768]{1,0:T(8,128)}) custom-call(bf16[640,2048]{1,0:T(8,128)(2,1)} %bitcast.102, bf16[1,2048,768]{2,1,0:T(8,128)(2,1)} %wg_ref.3, bf16[1,2048,768]{2,1,0:T(8,128)(2,1)} %wu_ref.3), custom_call_target="tpu_custom_call" | custom-call | flops 4026531840 | bytes 16000000 | tf_op jit(solution)/shard_map/pallas_call | solution.py:107
  70.9 18.5 %all-to-all-done = bf16[16,40,2048]{2,1,0:T(8,128)(2,1)} async-done(((bf16[16,40,2048]{2,1,0:T(8,128)(2,1)}), bf16[16,40,2048]{2,1,0:T(8,128)(2,1)}, u32[]{:S(2)}, u32[]{:S(2)}) %all-to-all-start) | async-done | bytes 2621472 | tf_op jit(solution)/shard_map/all_to_all | solution.py:279
  90.9 6.9 %shard_map.113 = (bf16[640,768]{1,0:T(8,128)(2,1)}, bf16[640,768]{1,0:T(8,128)(2,1)}, bf16[640,128]{1,0:T(8,128)(2,1)S(1)}) custom-call(s32[1]{0:T(128)} %bitcast.2.me_ref, bf16[640,2048]{1,0:T(8,128)(2,1)} %bitcast.4.dy_ref, bf16[1,768,2048]{2,1,0:T(8,128)(2,1)} %wd_ref.1, f32[640,768]{1,0:T(8,128)S(1)} %get-tuple-element.14.h_ref, ...), custom_call_target="tpu_custom_call" | custom-call | flops 2013265920 | bytes 14000000 | tf_op jit(solution)/shard_map/pallas_call | solution.py:168
  97.8 3.5 %constant_dynamic-slice_fusion = (bf16[640,1024]{1,0:T(8,128)(2,1)}, bf16[640,1024]{1,0:T(8,128)(2,1)}) fusion(bf16[640,2048]{1,0:T(8,128)(2,1)} %bitcast.4.dy_ref, s32[]{:T(128)S(6)} %select_n.88, s32[]{:T(128)S(6)} %select_n.87), kind=kLoop, calls=%fused_computation.52 | loop fusion | bytes 5242888 | tf_op jit(solution)/shard_map/dynamic_slice | solution.py:326
  102.3 7.1 %shard_map.114 = bf16[640,2176]{1,0:T(8,128)(2,1)S(1)} custom-call(bf16[640,768]{1,0:T(8,128)(2,1)} %get-tuple-element.17.dg_ref.a_ref, bf16[640,768]{1,0:T(8,128)(2,1)} %get-tuple-element.18.du_ref.a_ref, bf16[1,2048,768]{2,1,0:T(8,128)(2,1)} %wg_ref.3, bf16[1,2048,768]{2,1,0:T(8,128)(2,1)} %wu_ref.3, bf16[640,128]{1,0:T(8,128)(2,1)S(1)} %get-tuple-element.19.gg_ref), custom_call_target="tpu_custom_call" | custom-call | flops 4026531840 | bytes 12000000 | tf_op jit(solution)/shard_map/pallas_call | solution.py:206
  110.9 8.7 %all-to-all-start.2 = ((bf16[16,40,2176]{2,1,0:T(8,128)(2,1)}), bf16[16,40,2176]{2,1,0:T(8,128)(2,1)S(1)}, u32[]{:S(2)}, u32[]{:S(2)}) async-start(bf16[16,40,2176]{2,1,0:T(8,128)(2,1)} %bitcast.105), calls=%async_computation.2 | async-start | bytes 5570560 | tf_op jit(solution)/shard_map/all_to_all | solution.py:279
  121.0 4.7 %shard_map.117 = bf16[1024,768]{1,0:T(8,128)(2,1)S(1)} custom-call(bf16[1024,640]{1,0:T(8,128)(2,1)S(1)} %bitcast.130, bf16[1024,640]{1,0:T(8,128)(2,1)} %bitcast.12.bt_ref, bf16[640,768]{1,0:T(8,128)(2,1)} %get-tuple-element.17.dg_ref.a_ref, bf16[640,768]{1,0:T(8,128)(2,1)} %collective-permute-done.1.b_ref), custom_call_target="tpu_custom_call" | custom-call | flops 2013265920 | bytes 6160384 | tf_op jit(solution)/shard_map/pallas_call | solution.py:226
  125.7 2.0 %collective-permute-start.2 = (bf16[128,768]{1,0:T(8,128)(2,1)S(1)}, bf16[128,768]{1,0:T(8,128)(2,1)S(1)}, u32[]{:S(2)}, u32[]{:S(2)}) collective-permute-start(bf16[128,768]{1,0:T(8,128)(2,1)S(1)} %dynamic-slice_bitcast_fusion.3), channel_id=1, source_target_pairs={{0,32},{16,240},{32,64},{48,16},{64,96},{80,48},{96,128},{112,80},... | collective-permute-start | bytes 589832 | tf_op jit(solution)/shard_map/ppermute | solution.py:302
  127.7 4.7 %shard_map.118 = bf16[1024,768]{1,0:T(8,128)(2,1)S(1)} custom-call(bf16[1024,640]{1,0:T(8,128)(2,1)S(1)} %bitcast.131, bf16[1024,640]{1,0:T(8,128)(2,1)} %bitcast.12.bt_ref, bf16[640,768]{1,0:T(8,128)(2,1)} %get-tuple-element.18.du_ref.a_ref, bf16[640,768]{1,0:T(8,128)(2,1)} %collective-permute-done.9.b_ref), custom_call_target="tpu_custom_call" | custom-call | flops 2013265920 | bytes 6160384 | tf_op jit(solution)/shard_map/pallas_call | solution.py:226
  132.4 2.1 %collective-permute-start.10 = (bf16[128,768]{1,0:T(8,128)(2,1)S(1)}, bf16[128,768]{1,0:T(8,128)(2,1)S(1)}, u32[]{:S(2)}, u32[]{:S(2)}) collective-permute-start(bf16[128,768]{1,0:T(8,128)(2,1)S(1)} %dynamic-slice_bitcast_fusion.2), channel_id=1, source_target_pairs={{0,32},{16,240},{32,64},{48,16},{64,96},{80,48},{96,128},{112,80},... | collective-permute-start | bytes 589832 | tf_op jit(solution)/shard_map/ppermute | solution.py:302
  134.5 5.2 %shard_map.119 = bf16[768,1024]{1,0:T(8,128)(2,1)S(1)} custom-call(bf16[768,640]{1,0:T(8,128)(2,1)} %get-tuple-element.22.at_ref, bf16[768,640]{1,0:T(8,128)(2,1)} %collective-permute-done.17.bt_ref, bf16[640,1024]{1,0:T(8,128)(2,1)S(1)} %copy-done.10, bf16[640,1024]{1,0:T(8,128)(2,1)} %collective-permute-done.18.b_ref), custom_call_target="tpu_custom_call" | custom-call | flops 2013265920 | bytes 6160384 | tf_op jit(solution)/shard_map/pallas_call | solution.py:226
  139.8 2.0 %collective-permute-start.19 = (bf16[96,1024]{1,0:T(8,128)(2,1)S(1)}, bf16[96,1024]{1,0:T(8,128)(2,1)S(1)}, u32[]{:S(2)}, u32[]{:S(2)}) collective-permute-start(bf16[96,1024]{1,0:T(8,128)(2,1)S(1)} %dynamic-slice_bitcast_fusion.1), channel_id=1, source_target_pairs={{0,32},{16,240},{32,64},{48,16},{64,96},{80,48},{96,128},{112,80},... | collective-permute-start | bytes 589832 | tf_op jit(solution)/shard_map/ppermute | solution.py:302
  141.9 3.3 %collective-permute-start.3 = (bf16[128,768]{1,0:T(8,128)(2,1)S(1)}, bf16[128,768]{1,0:T(8,128)(2,1)S(1)}, u32[]{:S(2)}, u32[]{:S(2)}) collective-permute-start(bf16[128,768]{1,0:T(8,128)(2,1)S(1)} %fusion.20), channel_id=1, source_target_pairs={{0,32},{16,240},{32,64},{48,16},{64,96},{80,48},{96,128},{112,80},... | collective-permute-start | bytes 589832 | tf_op jit(solution)/shard_map/ppermute | solution.py:302
  148.9 2.0 %collective-permute-start.4 = (bf16[128,768]{1,0:T(8,128)(2,1)S(1)}, bf16[128,768]{1,0:T(8,128)(2,1)S(1)}, u32[]{:S(2)}, u32[]{:S(2)}) collective-permute-start(bf16[128,768]{1,0:T(8,128)(2,1)S(1)} %fusion.19), channel_id=1, source_target_pairs={{0,32},{16,240},{32,64},{48,16},{64,96},{80,48},{96,128},{112,80},... | collective-permute-start | bytes 589832 | tf_op jit(solution)/shard_map/ppermute | solution.py:302
  159.3 1.9 collective-permute-done.21
  163.6 2.6 %collective-permute-done.13 = bf16[128,768]{1,0:T(8,128)(2,1)S(1)} collective-permute-done((bf16[128,768]{1,0:T(8,128)(2,1)S(1)}, bf16[128,768]{1,0:T(8,128)(2,1)S(1)}, u32[]{:S(2)}, u32[]{:S(2)}) %collective-permute-start.13) | collective-permute-done | bytes 196640 | tf_op jit(solution)/shard_map/ppermute | solution.py:302
  166.3 2.0 %collective-permute-done.22 = bf16[96,1024]{1,0:T(8,128)(2,1)S(1)} collective-permute-done((bf16[96,1024]{1,0:T(8,128)(2,1)S(1)}, bf16[96,1024]{1,0:T(8,128)(2,1)S(1)}, u32[]{:S(2)}, u32[]{:S(2)}) %collective-permute-start.22) | collective-permute-done | bytes 196640 | tf_op jit(solution)/shard_map/ppermute | solution.py:302
  170.6 2.6 %collective-permute-done.14 = bf16[128,768]{1,0:T(8,128)(2,1)S(1)} collective-permute-done((bf16[128,768]{1,0:T(8,128)(2,1)S(1)}, bf16[128,768]{1,0:T(8,128)(2,1)S(1)}, u32[]{:S(2)}, u32[]{:S(2)}) %collective-permute-start.14) | collective-permute-done | bytes 196640 | tf_op jit(solution)/shard_map/ppermute | solution.py:302
  177.8 2.6 %collective-permute-done.15 = bf16[128,768]{1,0:T(8,128)(2,1)S(1)} collective-permute-done((bf16[128,768]{1,0:T(8,128)(2,1)S(1)}, bf16[128,768]{1,0:T(8,128)(2,1)S(1)}, u32[]{:S(2)}, u32[]{:S(2)}) %collective-permute-start.15) | collective-permute-done | bytes 196640 | tf_op jit(solution)/shard_map/ppermute | solution.py:302
  183.7 2.8 %shard_map.115 = (bf16[128,2048]{1,0:T(8,128)(2,1)}, f32[4,128]{1,0:T(4,128)S(1)}) custom-call(s32[4,128]{1,0:T(4,128)S(1)} %bitcast.134, bf16[4,128]{1,0:T(4,128)(2,1)S(1)} %bitcast.136, bf16[640,2176]{1,0:T(8,128)(2,1)S(1)} %bitcast.99, bf16[640,2176]{1,0:T(8,128)(2,1)S(1)} %bitcast.100), custom_call_target="tpu_custom_call" | custom-call | flops 335544320 | bytes 2621440 | tf_op jit(solution)/shard_map/pallas_call | solution.py:257
  187.0 3.4 %collective-permute-done.25 = bf16[96,1024]{1,0:T(8,128)(2,1)} collective-permute-done((bf16[96,1024]{1,0:T(8,128)(2,1)}, bf16[96,1024]{1,0:T(8,128)(2,1)}, u32[]{:S(2)}, u32[]{:S(2)}) %collective-permute-start.25) | collective-permute-done | bytes 196640 | tf_op jit(solution)/shard_map/ppermute | solution.py:302
  (108 shorter events, 49.2 us)
Async XLA Ops:
  5.5 42.4 %all-to-all-start.1 = ((bf16[16,40,2048]{2,1,0:T(8,128)(2,1)}), bf16[16,40,2048]{2,1,0:T(8,128)(2,1)S(1)}, u32[]{:S(2)}, u32[]{:S(2)}) async-start(bf16[16,40,2048]{2,1,0:T(8,128)(2,1)} %bitcast.104), calls=%async_computation.1 | async-start | bytes 5242880 | tf_op jit(solution)/shard_map/all_to_all | solution.py:279
  47.9 41.4 %all-to-all-start = ((bf16[16,40,2048]{2,1,0:T(8,128)(2,1)}), bf16[16,40,2048]{2,1,0:T(8,128)(2,1)}, u32[]{:S(2)}, u32[]{:S(2)}) async-start(bf16[16,40,2048]{2,1,0:T(8,128)(2,1)} %bitcast.103), calls=%async_computation | async-start | bytes 5242880 | tf_op jit(solution)/shard_map/all_to_all | solution.py:279
  60.9 58.8 %collective-permute-start = (bf16[8,128,640]{2,1,0:T(8,128)(2,1)}, bf16[8,128,640]{2,1,0:T(8,128)(2,1)}, u32[]{:S(2)}, u32[]{:S(2)}) collective-permute-start(bf16[8,128,640]{2,1,0:T(8,128)(2,1)} %get-tuple-element.25), channel_id=1, source_target_pairs={{0,16},{16,0},{32,48},{48,32},{64,80},{80,64},{96,112},{112,96},{1... | collective-permute-start | bytes 3932168 | tf_op jit(solution)/shard_map/ppermute | solution.py:286
  97.8 21.9 %collective-permute-start.1 = (bf16[640,768]{1,0:T(8,128)(2,1)}, bf16[640,768]{1,0:T(8,128)(2,1)}, u32[]{:S(2)}, u32[]{:S(2)}) collective-permute-start(bf16[640,768]{1,0:T(8,128)(2,1)} %get-tuple-element.17.dg_ref.a_ref), channel_id=1, source_target_pairs={{0,16},{16,0},{32,48},{48,32},{64,80},{80,64},{96,112},{112,96},{1... | collective-permute-start | bytes 2949128 | tf_op jit(solution)/shard_map/ppermute | solution.py:286
  101.3 33.3 %collective-permute-start.18 = (bf16[640,1024]{1,0:T(8,128)(2,1)}, bf16[640,1024]{1,0:T(8,128)(2,1)}, u32[]{:S(2)}, u32[]{:S(2)}) collective-permute-start(bf16[640,1024]{1,0:T(8,128)(2,1)} %get-tuple-element.23), channel_id=1, source_target_pairs={{0,16},{16,0},{32,48},{48,32},{64,80},{80,64},{96,112},{112,96},{1... | collective-permute-start | bytes 3932168 | tf_op jit(solution)/shard_map/ppermute | solution.py:286
  101.8 25.9 %collective-permute-start.9 = (bf16[640,768]{1,0:T(8,128)(2,1)}, bf16[640,768]{1,0:T(8,128)(2,1)}, u32[]{:S(2)}, u32[]{:S(2)}) collective-permute-start(bf16[640,768]{1,0:T(8,128)(2,1)} %get-tuple-element.18.du_ref.a_ref), channel_id=1, source_target_pairs={{0,16},{16,0},{32,48},{48,32},{64,80},{80,64},{96,112},{112,96},{1... | collective-permute-start | bytes 2949128 | tf_op jit(solution)/shard_map/ppermute | solution.py:286
  101.8 32.8 %collective-permute-start.17 = (bf16[768,640]{1,0:T(8,128)(2,1)}, bf16[768,640]{1,0:T(8,128)(2,1)}, u32[]{:S(2)}, u32[]{:S(2)}) collective-permute-start(bf16[768,640]{1,0:T(8,128)(2,1)} %get-tuple-element.22.at_ref), channel_id=1, source_target_pairs={{0,16},{16,0},{32,48},{48,32},{64,80},{80,64},{96,112},{112,96},{1... | collective-permute-start | bytes 2949128 | tf_op jit(solution)/shard_map/ppermute | solution.py:286
  110.9 72.8 %all-to-all-start.2 = ((bf16[16,40,2176]{2,1,0:T(8,128)(2,1)}), bf16[16,40,2176]{2,1,0:T(8,128)(2,1)S(1)}, u32[]{:S(2)}, u32[]{:S(2)}) async-start(bf16[16,40,2176]{2,1,0:T(8,128)(2,1)} %bitcast.105), calls=%async_computation.2 | async-start | bytes 5570560 | tf_op jit(solution)/shard_map/all_to_all | solution.py:279
  125.7 16.1 %collective-permute-start.2 = (bf16[128,768]{1,0:T(8,128)(2,1)S(1)}, bf16[128,768]{1,0:T(8,128)(2,1)S(1)}, u32[]{:S(2)}, u32[]{:S(2)}) collective-permute-start(bf16[128,768]{1,0:T(8,128)(2,1)S(1)} %dynamic-slice_bitcast_fusion.3), channel_id=1, source_target_pairs={{0,32},{16,240},{32,64},{48,16},{64,96},{80,48},{96,128},{112,80},... | collective-permute-start | bytes 589832 | tf_op jit(solution)/shard_map/ppermute | solution.py:302
  132.4 12.7 %collective-permute-start.10 = (bf16[128,768]{1,0:T(8,128)(2,1)S(1)}, bf16[128,768]{1,0:T(8,128)(2,1)S(1)}, u32[]{:S(2)}, u32[]{:S(2)}) collective-permute-start(bf16[128,768]{1,0:T(8,128)(2,1)S(1)} %dynamic-slice_bitcast_fusion.2), channel_id=1, source_target_pairs={{0,32},{16,240},{32,64},{48,16},{64,96},{80,48},{96,128},{112,80},... | collective-permute-start | bytes 589832 | tf_op jit(solution)/shard_map/ppermute | solution.py:302
  139.8 7.0 %collective-permute-start.19 = (bf16[96,1024]{1,0:T(8,128)(2,1)S(1)}, bf16[96,1024]{1,0:T(8,128)(2,1)S(1)}, u32[]{:S(2)}, u32[]{:S(2)}) collective-permute-start(bf16[96,1024]{1,0:T(8,128)(2,1)S(1)} %dynamic-slice_bitcast_fusion.1), channel_id=1, source_target_pairs={{0,32},{16,240},{32,64},{48,16},{64,96},{80,48},{96,128},{112,80},... | collective-permute-start | bytes 589832 | tf_op jit(solution)/shard_map/ppermute | solution.py:302
  141.9 7.0 %collective-permute-start.3 = (bf16[128,768]{1,0:T(8,128)(2,1)S(1)}, bf16[128,768]{1,0:T(8,128)(2,1)S(1)}, u32[]{:S(2)}, u32[]{:S(2)}) collective-permute-start(bf16[128,768]{1,0:T(8,128)(2,1)S(1)} %fusion.20), channel_id=1, source_target_pairs={{0,32},{16,240},{32,64},{48,16},{64,96},{80,48},{96,128},{112,80},... | collective-permute-start | bytes 589832 | tf_op jit(solution)/shard_map/ppermute | solution.py:302
  145.2 7.0 %collective-permute-start.11 = (bf16[128,768]{1,0:T(8,128)(2,1)S(1)}, bf16[128,768]{1,0:T(8,128)(2,1)S(1)}, u32[]{:S(2)}, u32[]{:S(2)}) collective-permute-start(bf16[128,768]{1,0:T(8,128)(2,1)S(1)} %fusion.13), channel_id=1, source_target_pairs={{0,32},{16,240},{32,64},{48,16},{64,96},{80,48},{96,128},{112,80},... | collective-permute-start | bytes 589832 | tf_op jit(solution)/shard_map/ppermute | solution.py:302
  146.8 7.4 %collective-permute-start.20 = (bf16[96,1024]{1,0:T(8,128)(2,1)S(1)}, bf16[96,1024]{1,0:T(8,128)(2,1)S(1)}, u32[]{:S(2)}, u32[]{:S(2)}) collective-permute-start(bf16[96,1024]{1,0:T(8,128)(2,1)S(1)} %fusion.6), channel_id=1, source_target_pairs={{0,32},{16,240},{32,64},{48,16},{64,96},{80,48},{96,128},{112,80},... | collective-permute-start | bytes 589832 | tf_op jit(solution)/shard_map/ppermute | solution.py:302
  148.9 7.4 %collective-permute-start.4 = (bf16[128,768]{1,0:T(8,128)(2,1)S(1)}, bf16[128,768]{1,0:T(8,128)(2,1)S(1)}, u32[]{:S(2)}, u32[]{:S(2)}) collective-permute-start(bf16[128,768]{1,0:T(8,128)(2,1)S(1)} %fusion.19), channel_id=1, source_target_pairs={{0,32},{16,240},{32,64},{48,16},{64,96},{80,48},{96,128},{112,80},... | collective-permute-start | bytes 589832 | tf_op jit(solution)/shard_map/ppermute | solution.py:302
  156.4 7.0 %collective-permute-start.5 = (bf16[128,768]{1,0:T(8,128)(2,1)S(1)}, bf16[128,768]{1,0:T(8,128)(2,1)S(1)}, u32[]{:S(2)}, u32[]{:S(2)}) collective-permute-start(bf16[128,768]{1,0:T(8,128)(2,1)S(1)} %fusion.18), channel_id=1, source_target_pairs={{0,32},{16,240},{32,64},{48,16},{64,96},{80,48},{96,128},{112,80},... | collective-permute-start | bytes 589832 | tf_op jit(solution)/shard_map/ppermute | solution.py:302
  159.2 7.0 %collective-permute-start.13 = (bf16[128,768]{1,0:T(8,128)(2,1)S(1)}, bf16[128,768]{1,0:T(8,128)(2,1)S(1)}, u32[]{:S(2)}, u32[]{:S(2)}) collective-permute-start(bf16[128,768]{1,0:T(8,128)(2,1)S(1)} %fusion.11), channel_id=1, source_target_pairs={{0,32},{16,240},{32,64},{48,16},{64,96},{80,48},{96,128},{112,80},... | collective-permute-start | bytes 589832 | tf_op jit(solution)/shard_map/ppermute | solution.py:302
  163.4 7.0 %collective-permute-start.6 = (bf16[128,768]{1,0:T(8,128)(2,1)S(1)}, bf16[128,768]{1,0:T(8,128)(2,1)S(1)}, u32[]{:S(2)}, u32[]{:S(2)}) collective-permute-start(bf16[128,768]{1,0:T(8,128)(2,1)S(1)} %fusion.17), channel_id=1, source_target_pairs={{0,32},{16,240},{32,64},{48,16},{64,96},{80,48},{96,128},{112,80},... | collective-permute-start | bytes 589832 | tf_op jit(solution)/shard_map/ppermute | solution.py:302
  170.4 7.0 %collective-permute-start.7 = (bf16[128,768]{1,0:T(8,128)(2,1)S(1)}, bf16[128,768]{1,0:T(8,128)(2,1)S(1)}, u32[]{:S(2)}, u32[]{:S(2)}) collective-permute-start(bf16[128,768]{1,0:T(8,128)(2,1)S(1)} %fusion.16), channel_id=1, source_target_pairs={{0,32},{16,240},{32,64},{48,16},{64,96},{80,48},{96,128},{112,80},... | collective-permute-start | bytes 589832 | tf_op jit(solution)/shard_map/ppermute | solution.py:302
  173.2 7.2 %collective-permute-start.15 = (bf16[128,768]{1,0:T(8,128)(2,1)S(1)}, bf16[128,768]{1,0:T(8,128)(2,1)S(1)}, u32[]{:S(2)}, u32[]{:S(2)}) collective-permute-start(bf16[128,768]{1,0:T(8,128)(2,1)S(1)} %fusion.9), channel_id=1, source_target_pairs={{0,32},{16,240},{32,64},{48,16},{64,96},{80,48},{96,128},{112,80},... | collective-permute-start | bytes 589832 | tf_op jit(solution)/shard_map/ppermute | solution.py:302
  175.3 7.2 %collective-permute-start.24 = (bf16[96,1024]{1,0:T(8,128)(2,1)S(1)}, bf16[96,1024]{1,0:T(8,128)(2,1)S(1)}, u32[]{:S(2)}, u32[]{:S(2)}) collective-permute-start(bf16[96,1024]{1,0:T(8,128)(2,1)S(1)} %fusion.2), channel_id=1, source_target_pairs={{0,32},{16,240},{32,64},{48,16},{64,96},{80,48},{96,128},{112,80},... | collective-permute-start | bytes 589832 | tf_op jit(solution)/shard_map/ppermute | solution.py:302
  177.4 14.2 %collective-permute-start.8 = (bf16[128,768]{1,0:T(8,128)(2,1)S(1)}, bf16[128,768]{1,0:T(8,128)(2,1)S(1)}, u32[]{:S(2)}, u32[]{:S(2)}) collective-permute-start(bf16[128,768]{1,0:T(8,128)(2,1)S(1)} %fusion.15), channel_id=1, source_target_pairs={{0,32},{16,240},{32,64},{48,16},{64,96},{80,48},{96,128},{112,80},... | collective-permute-start | bytes 589832 | tf_op jit(solution)/shard_map/ppermute | solution.py:302
  181.1 12.2 %collective-permute-start.16 = (bf16[128,768]{1,0:T(8,128)(2,1)}, bf16[128,768]{1,0:T(8,128)(2,1)S(1)}, u32[]{:S(2)}, u32[]{:S(2)}) collective-permute-start(bf16[128,768]{1,0:T(8,128)(2,1)} %fusion.8), channel_id=1, source_target_pairs={{0,32},{16,240},{32,64},{48,16},{64,96},{80,48},{96,128},{112,80},... | collective-permute-start | bytes 589832 | tf_op jit(solution)/shard_map/ppermute | solution.py:302
  183.2 7.2 %collective-permute-start.25 = (bf16[96,1024]{1,0:T(8,128)(2,1)}, bf16[96,1024]{1,0:T(8,128)(2,1)}, u32[]{:S(2)}, u32[]{:S(2)}) collective-permute-start(bf16[96,1024]{1,0:T(8,128)(2,1)} %fusion.1), channel_id=1, source_target_pairs={{0,32},{16,240},{32,64},{48,16},{64,96},{80,48},{96,128},{112,80},... | collective-permute-start | bytes 589832 | tf_op jit(solution)/shard_map/ppermute | solution.py:302
  (22 other events, 232.3 us)

commit v2 on v1

v2 whole, which is shorter than its diff:
```python
import jax
import jax.numpy as jnp
from jax import lax
from jax.experimental import pallas as pl
from jax.experimental.pallas import tpu as pltpu
from jax.sharding import PartitionSpec as P

F32 = jnp.float32
BF16 = jnp.bfloat16
N_TOK = 128
D = 2048
FF = 768
CAP = 40
N_EXP = 16
ROWS = N_EXP * CAP
N_Z = 8
EXTRA = 128
H = D // 2
Q = D // 4


def params(mib=60):
    return pltpu.CompilerParams(vmem_limit_bytes=mib * 1024 * 1024)


def cost(flops, nbytes):
    return pl.CostEstimate(flops=int(flops), bytes_accessed=int(nbytes), transcendentals=0)


def dot(a, b, ca=1, cb=0):
    return lax.dot_general(a, b, (((ca,), (cb,)), ((), ())), preferred_element_type=F32)


def slot_matrix(ids_t, gates_t=None):
    expert = lax.broadcasted_iota(jnp.int32, (N_EXP, N_TOK), 0)
    member = jnp.zeros((N_EXP, N_TOK), F32)
    weight = jnp.zeros((N_EXP, N_TOK), F32)
    for k in range(4):
        hit = ids_t[k : k + 1, :] == expert
        member = jnp.where(hit, 1.0, member)
        if gates_t is not None:
            weight = jnp.where(hit, gates_t[k : k + 1, :].astype(F32), weight)
    row = lax.broadcasted_iota(jnp.int32, (N_TOK, N_TOK), 0)
    col = lax.broadcasted_iota(jnp.int32, (N_TOK, N_TOK), 1)
    before = jnp.where(row < col, 1.0, 0.0).astype(BF16)
    position = dot(member.astype(BF16), before)
    code = jnp.where(member > 0.0, position, -1.0)
    slot = lax.broadcasted_iota(jnp.int32, (CAP, N_TOK), 0).astype(F32)
    pieces = []
    for e in range(N_EXP):
        value = 1.0 if gates_t is None else weight[e : e + 1, :]
        pieces.append(jnp.where(code[e : e + 1, :] == slot, value, 0.0))
    return jnp.concatenate(pieces, axis=0).astype(BF16)


def first_dispatch_kernel(core_ref, ids_ref, gates_ref, x_ref, dy_ref, out_ref, slots, gated):
    n = pl.program_id(0)

    @pl.when(n == 0)
    def _():
        slots[...] = slot_matrix(ids_ref[...])
        gated[...] = slot_matrix(ids_ref[...], gates_ref[...])

    @pl.when(n < 4)
    def _():
        out_ref[...] = dot(slots[...], x_ref[...]).astype(BF16)

    @pl.when(n >= 4)
    def _():
        out_ref[...] = dot(gated[...], dy_ref[...]).astype(BF16)


def first_dispatch(core, ids_t, gates_t, x, dy):
    small = pl.BlockSpec((4, N_TOK), lambda n, c: (0, 0))
    mask = pltpu.VMEM((ROWS, N_TOK), BF16)

    def quarter(n, c):
        return 0, jnp.where(n == 5, 2 * (1 - c[0]), 2 * c[0])

    return pl.pallas_call(
        first_dispatch_kernel,
        grid_spec=pltpu.PrefetchScalarGridSpec(
            num_scalar_prefetch=1,
            grid=(6,),
            in_specs=[
                small,
                small,
                pl.BlockSpec((N_TOK, Q), lambda n, c: (0, jnp.minimum(n, 3))),
                pl.BlockSpec((N_TOK, Q), quarter),
            ],
            out_specs=pl.BlockSpec((ROWS, Q), lambda n, c: (0, n)),
            scratch_shapes=[mask, mask],
        ),
        out_shape=jax.ShapeDtypeStruct((ROWS, D + H), BF16),
        compiler_params=params(),
        cost_estimate=cost(2 * ROWS * N_TOK * 3072, 2 * ROWS * 3072),
    )(core, ids_t, gates_t, x, dy)


def second_dispatch_kernel(core_ref, ids_ref, gates_ref, dy_ref, out_ref, gated):
    @pl.when(pl.program_id(0) == 0)
    def _():
        gated[...] = slot_matrix(ids_ref[...], gates_ref[...])

    out_ref[...] = dot(gated[...], dy_ref[...]).astype(BF16)


def second_dispatch(core, ids_t, gates_t, dy):
    small = pl.BlockSpec((4, N_TOK), lambda n, c: (0, 0))

    def quarter(n, c):
        return 0, jnp.where(n == 1, 2 * (1 - c[0]), 2 * c[0]) + 1

    return pl.pallas_call(
        second_dispatch_kernel,
        grid_spec=pltpu.PrefetchScalarGridSpec(
            num_scalar_prefetch=1,
            grid=(2,),
            in_specs=[small, small, pl.BlockSpec((N_TOK, Q), quarter)],
            out_specs=pl.BlockSpec((ROWS, Q), lambda n, c: (0, n)),
            scratch_shapes=[pltpu.VMEM((ROWS, N_TOK), BF16)],
        ),
        out_shape=jax.ShapeDtypeStruct((ROWS, H), BF16),
        compiler_params=params(),
        cost_estimate=cost(2 * ROWS * N_TOK * H, 2 * ROWS * H),
    )(core, ids_t, gates_t, dy)


def down_turn_kernel(core_ref, w_ref, out_ref):
    out_ref[...] = w_ref[0].T


def turn_down(core, w):
    def quarter(n, c):
        own = 2 * c[0]
        other = 2 * (1 - c[0])
        return 0, 0, jnp.where(n % 2 == 0, own, other) + n // 2

    return pl.pallas_call(
        down_turn_kernel,
        grid_spec=pltpu.PrefetchScalarGridSpec(
            num_scalar_prefetch=1,
            grid=(4,),
            in_specs=[pl.BlockSpec((1, FF, Q), quarter)],
            out_specs=pl.BlockSpec((Q, FF), lambda n, c: (n, 0)),
        ),
        out_shape=jax.ShapeDtypeStruct((D, FF), BF16),
        compiler_params=params(),
        cost_estimate=cost(0, 4 * D * FF),
    )(core, w)


def up_turn_kernel(g_ref, u_ref, gt_ref, ut_ref):
    gt_ref[...] = g_ref[0].T
    ut_ref[...] = u_ref[0].T


def turn_up(wg, wu):
    weight = pl.BlockSpec((1, Q, FF), lambda n: (0, n, 0))
    out = pl.BlockSpec((FF, Q), lambda n: (0, n))
    shape = jax.ShapeDtypeStruct((FF, D), BF16)
    return pl.pallas_call(
        up_turn_kernel,
        grid=(4,),
        in_specs=[weight, weight],
        out_specs=[out, out],
        out_shape=[shape, shape],
        compiler_params=params(),
        cost_estimate=cost(0, 8 * D * FF),
    )(wg, wu)


def forward_kernel(x_ref, dy_ref, wg_ref, wu_ref, wd_ref, ht_ref, h_ref, f_ref, a_ref, b_ref):
    x = x_ref[...]
    g = dot(x, wg_ref[0])
    u = dot(x, wu_ref[0])
    s = jax.nn.sigmoid(g)
    a = g * s
    h = a * u
    h_ref[...] = h
    ht_ref[...] = h.T.astype(BF16)
    a_ref[...] = a
    f_ref[...] = u * s * (1.0 + g * (1.0 - s))
    b_ref[...] = dot(dy_ref[...], wd_ref[...])


def forward(first, wg, wu, wd_t):
    width = 256
    full = jax.ShapeDtypeStruct((ROWS, FF), F32)
    out = pl.BlockSpec((ROWS, width), lambda n: (0, n))
    return pl.pallas_call(
        forward_kernel,
        grid=(FF // width,),
        in_specs=[
            pl.BlockSpec((ROWS, D), lambda n: (0, 0)),
            pl.BlockSpec((ROWS, H), lambda n: (0, 2)),
            pl.BlockSpec((1, D, width), lambda n: (0, 0, n)),
            pl.BlockSpec((1, D, width), lambda n: (0, 0, n)),
            pl.BlockSpec((H, width), lambda n: (0, n)),
        ],
        out_specs=[pl.BlockSpec((width, ROWS), lambda n: (n, 0)), out, out, out, out],
        out_shape=[jax.ShapeDtypeStruct((FF, ROWS), BF16), full, full, full, full],
        compiler_params=params(),
        cost_estimate=cost(5 * ROWS * D * FF, 20_000_000),
    )(first, first, wg, wu, wd_t)


def split_kernel(core_ref, mine_ref, theirs_ref, own_ref, other_ref):
    own_ref[...] = mine_ref[...].T
    other_ref[...] = theirs_ref[...].T


def split_transposed(core, first):
    shape = jax.ShapeDtypeStruct((H, ROWS), BF16)
    out = pl.BlockSpec((128, ROWS), lambda n, c: (n, 0))
    return pl.pallas_call(
        split_kernel,
        grid_spec=pltpu.PrefetchScalarGridSpec(
            num_scalar_prefetch=1,
            grid=(N_Z,),
            in_specs=[
                pl.BlockSpec((ROWS, 128), lambda n, c: (0, 2 * n + c[0])),
                pl.BlockSpec((ROWS, 128), lambda n, c: (0, 2 * n + 1 - c[0])),
            ],
            out_specs=[out, out],
        ),
        out_shape=[shape, shape],
        compiler_params=params(),
        cost_estimate=cost(0, 4 * ROWS * D),
    )(core, first, first)


def backward_kernel(me_ref, dy_ref, wd_ref, h_ref, f_ref, a_ref, b_ref, dg_ref, du_ref, gg_ref, total):
    n = pl.program_id(0)
    b = b_ref[...] + dot(dy_ref[...], wd_ref[...])
    dg_ref[...] = (b * f_ref[...]).astype(BF16)
    du_ref[...] = (b * a_ref[...]).astype(BF16)
    part = jnp.sum(b * h_ref[...], axis=1, keepdims=True)
    part = jnp.broadcast_to(part, (ROWS, EXTRA))

    @pl.when(n == 0)
    def _():
        total[...] = part

    @pl.when(n > 0)
    def _():
        total[...] += part

    @pl.when(n == pl.num_programs(0) - 1)
    def _():
        value = total[...]
        high = value.astype(BF16).astype(F32)
        col = lax.broadcasted_iota(jnp.int32, (ROWS, EXTRA), 1)
        me = me_ref[0]
        low = jnp.where(col == me + N_EXP, value - high, 0.0)
        gg_ref[...] = jnp.where(col == me, high, low).astype(BF16)


def backward(me, second, wd_t, h, f, a, b):
    width = 256
    part = pl.BlockSpec((ROWS, width), lambda n: (0, n))
    return pl.pallas_call(
        backward_kernel,
        grid=(FF // width,),
        in_specs=[
            pl.BlockSpec(memory_space=pltpu.SMEM),
            pl.BlockSpec((ROWS, H), lambda n: (0, 0)),
            pl.BlockSpec((H, width), lambda n: (1, n)),
            part,
            part,
            part,
            part,
        ],
        out_specs=[part, part, pl.BlockSpec((ROWS, EXTRA), lambda n: (0, 0))],
        out_shape=[
            jax.ShapeDtypeStruct((ROWS, FF), BF16),
            jax.ShapeDtypeStruct((ROWS, FF), BF16),
            jax.ShapeDtypeStruct((ROWS, EXTRA), BF16),
        ],
        scratch_shapes=[pltpu.VMEM((ROWS, EXTRA), F32)],
        compiler_params=params(),
        cost_estimate=cost(ROWS * D * FF, 12_000_000),
    )(me, second, wd_t, h, f, a, b)


def pair_kernel(dg_ref, du_ref, wg_ref, wu_ref, gg_ref, after_ref, out_ref):
    n = pl.program_id(0)
    width = wg_ref.shape[1]
    value = dot(dg_ref[...], wg_ref[...]) + dot(du_ref[...], wu_ref[...])
    out_ref[:, pl.ds(pl.multiple_of(n * width, width), width)] = value.astype(BF16)

    @pl.when(n == 0)
    def _():
        out_ref[:, D:] = gg_ref[...]


def pair_grads(dg, du, wg_t, wu_t, gg, after):
    width = 512
    whole = pl.BlockSpec((ROWS, FF), lambda n: (0, 0))
    weight = pl.BlockSpec((FF, width), lambda n: (0, n))
    return pl.pallas_call(
        pair_kernel,
        grid=(D // width,),
        in_specs=[
            whole,
            whole,
            weight,
            weight,
            pl.BlockSpec((ROWS, EXTRA), lambda n: (0, 0)),
            pl.BlockSpec(memory_space=pl.ANY),
        ],
        out_specs=pl.BlockSpec((ROWS, D + EXTRA), lambda n: (0, 0)),
        out_shape=jax.ShapeDtypeStruct((ROWS, D + EXTRA), BF16),
        compiler_params=params(28),
        cost_estimate=cost(4 * ROWS * D * FF, 12_000_000),
    )(dg, du, wg_t, wu_t, gg, after)


def outer_kernel(at_ref, bt_ref, a_ref, b_ref, after_ref, out_ref):
    value = dot(at_ref[...], a_ref[...]) + dot(bt_ref[...], b_ref[...])
    out_ref[...] = value.astype(BF16)


def outer_sum(own_t, other_t, own, other, n, at, after, total=None):
    m, width = own_t.shape[0], 256
    own_at, other_at, out_at = (place // width for place in at)
    left = pl.BlockSpec((m, ROWS), lambda j: (0, 0))
    return pl.pallas_call(
        outer_kernel,
        grid=(n // width,),
        in_specs=[
            left,
            left,
            pl.BlockSpec((ROWS, width), lambda j: (0, j + own_at)),
            pl.BlockSpec((ROWS, width), lambda j: (0, j + other_at)),
            pl.BlockSpec(memory_space=pl.ANY),
        ],
        out_specs=pl.BlockSpec((m, width), lambda j: (0, j + out_at)),
        out_shape=jax.ShapeDtypeStruct((m, total or n), BF16),
        input_output_aliases={4: 0} if out_at else {},
        compiler_params=params(28),
        cost_estimate=cost(4 * ROWS * m * n, 2 * (m * n + 2 * ROWS * (m + n))),
    )(own_t, other_t, own, other, after)


def combine_kernel(ids_ref, gates_ref, rows_ref, extra_ref, tok_ref, gate_ref, slots):
    @pl.when(pl.program_id(0) == 0)
    def _():
        matrix = slot_matrix(ids_ref[...])
        slots[...] = matrix
        by_expert = dot(extra_ref[...], matrix, 0, 0)
        value = by_expert[:N_EXP] + by_expert[N_EXP : 2 * N_EXP]
        expert = lax.broadcasted_iota(jnp.int32, (N_EXP, N_TOK), 0)
        choice = lax.broadcasted_iota(jnp.int32, (4, N_TOK), 0)
        grads = jnp.zeros((4, N_TOK), F32)
        for k in range(4):
            mine = jnp.where(ids_ref[k : k + 1, :] == expert, value, 0.0)
            grads = jnp.where(choice == k, jnp.sum(mine, axis=0, keepdims=True), grads)
        gate_ref[...] = (grads / gates_ref[...].astype(F32)).astype(BF16)

    tok_ref[...] = dot(slots[...], rows_ref[...], 0, 0).astype(BF16)


def combine(ids_t, gates_t, rows):
    width = 512
    small = pl.BlockSpec((4, N_TOK), lambda n: (0, 0))
    return pl.pallas_call(
        combine_kernel,
        grid=(D // width,),
        in_specs=[
            small,
            small,
            pl.BlockSpec((ROWS, width), lambda n: (0, n)),
            pl.BlockSpec((ROWS, EXTRA), lambda n: (0, D // EXTRA)),
        ],
        out_specs=[pl.BlockSpec((N_TOK, width), lambda n: (0, n)), small],
        out_shape=[
            jax.ShapeDtypeStruct((N_TOK, D), BF16),
            jax.ShapeDtypeStruct((4, N_TOK), BF16),
        ],
        scratch_shapes=[pltpu.VMEM((ROWS, N_TOK), BF16)],
        compiler_params=params(28),
        cost_estimate=cost(2 * ROWS * N_TOK * D, 2 * ROWS * D),
    )(ids_t, gates_t, rows, rows)


def exchange_experts(rows):
    width = rows.shape[1]
    moved = lax.all_to_all(
        rows.reshape(N_EXP, CAP, width), "expert", split_axis=0, concat_axis=0, tiled=True
    )
    return moved.reshape(ROWS, width)


def hold_kernel(*refs):
    pass


def hold(a, *after, mib=60):
    place = pl.BlockSpec(memory_space=pl.ANY)
    return pl.pallas_call(
        hold_kernel,
        in_specs=[place] * (1 + len(after)),
        out_specs=place,
        out_shape=jax.ShapeDtypeStruct(a.shape, a.dtype),
        input_output_aliases={0: 0},
        compiler_params=params(mib),
    )(a, *after)


def swap_cores(a):
    return lax.ppermute(a, "dp", [(i, i ^ 1) for i in range(2 * N_Z)])


def pick(a, index):
    return lax.dynamic_index_in_dim(a, index, 0, keepdims=False)


ROUTE = tuple((2 * i, 2 * ((i + 1) % N_Z)) for i in range(N_Z)) + tuple(
    (2 * i + 1, 2 * ((i - 1) % N_Z) + 1) for i in range(N_Z)
)


def ring_step(g, held, z, sign, step):
    if step == 1:
        held = pick(g, (z - sign) & (N_Z - 1))
    came = lax.ppermute(held, "dp", ROUTE)
    block = pick(g, (z - (step + 1) * sign) & (N_Z - 1))
    return (came.astype(F32) + block.astype(F32)).astype(BF16)


def body(tokens, out_grad, gates, expert_ids, w_gate, w_up, w_down):
    dp = lax.axis_index("dp").astype(jnp.int32)
    z, core = dp >> 1, dp & 1
    sign = 1 - 2 * core
    core_arg = core.reshape(1)
    me = lax.axis_index("expert").astype(jnp.int32).reshape(1)
    ids_t, gates_t = expert_ids.T, gates.T

    second_rows = second_dispatch(core_arg, ids_t, gates_t, out_grad)
    first = exchange_experts(first_dispatch(core_arg, ids_t, gates_t, tokens, out_grad))
    down_t = turn_down(core_arg, w_down)
    gate_t, up_t = turn_up(w_gate, w_up)
    second = exchange_experts(hold(second_rows, first, down_t, gate_t))

    hidden_t, hidden, factor, active, back = forward(first, w_gate, w_up, down_t)
    hidden_other_t = swap_cores(hidden_t)
    first_other = swap_cores(first[:, D + Q :])
    x_own, x_theirs = split_transposed(core_arg, first)
    x_other = swap_cores(x_theirs)
    part_low = outer_sum(hidden_t, hidden_other_t, first, first_other, Q, (D, 0, 0), first, H)

    second = hold(second, part_low, x_other)
    second_other = swap_cores(second)
    d_gate, d_up, prob = backward(me, second, down_t, hidden, factor, active, back)
    d_gate_other, d_up_other = swap_cores(d_gate), swap_cores(d_up)
    part_down = outer_sum(
        hidden_t, hidden_other_t, second, second_other, Q, (0, Q, Q), part_low, H
    )
    pairs = pair_grads(d_gate, d_up, gate_t, up_t, prob, part_down)
    part_gate = outer_sum(x_own, x_other, d_gate, d_gate_other, FF, (0, 0, 0), pairs)
    part_up = outer_sum(x_own, x_other, d_up, d_up_other, FF, (0, 0, 0), pairs)
    pairs = hold(pairs, part_gate, part_up, mib=1)
    rows = exchange_experts(pairs)
    token_grad, gate_grad_t = combine(ids_t, gates_t, rows)

    part_down = part_down.reshape(N_Z, FF // N_Z, H)
    part_gate = part_gate.reshape(N_Z, D // (2 * N_Z), FF)
    part_up = part_up.reshape(N_Z, D // (2 * N_Z), FF)
    sum_down = sum_gate = sum_up = None
    for step in range(1, N_Z):
        sum_down = ring_step(part_down, sum_down, z, sign, step)
        sum_gate = ring_step(part_gate, sum_gate, z, sign, step)
        sum_up = ring_step(part_up, sum_up, z, sign, step)
        if step == 1:
            sum_down = hold(sum_down, pairs, mib=1)
        if step == 6:
            sum_down = hold(sum_down, token_grad, mib=1)

    halves = sum_down.reshape(2, FF // (2 * N_Z), H)
    mine = pick(halves, core)
    theirs = swap_cores(pick(halves, 1 - core))
    left = jnp.where(core == 0, mine, theirs)
    right = jnp.where(core == 0, theirs, mine)
    grad_down = jnp.concatenate([left, right], axis=1)
    return token_grad, gate_grad_t.T, sum_gate[None], sum_up[None], grad_down[None]


def solution(mesh):
    both = P(("dp", "expert"), None)
    weight = P("expert", None, None)
    grad = P("expert", "dp", None)
    return jax.shard_map(
        body,
        mesh=mesh,
        in_specs=(both, both, both, both, weight, weight, weight),
        out_specs=(both, both, grad, grad, grad),
        check_vma=False,
    )
```

time: 198 us -> 209 us (1.056)
  Pallas kernels: 45 us -> 69.7 us
  waiting for transfers between devices: 80.3 us -> 72.1 us
  local copies, waits for them, and re-layouts: 16 us -> 11.1 us
  other arithmetic: 7.94 us -> 5.52 us
  starting transfers between devices: 45.5 us -> 47.8 us
    pallas_call x6 -> x14, Pallas kernels: 19.6 us -> 39.6 us  [the longest x4 13.8 us: outer_sum(): pl.pallas_call(outer_kernel, grid=(n // width,), in_specs=[left, left, pl...]
    all_to_all x3, waiting for transfers between devices: 50 us -> 41.6 us  [exchange_experts(): lax.all_to_all(rows.reshape(N_EXP, CAP, width), 'expert', split_axis=0, c...]
    ppermute x21, starting transfers between devices: 18.8 us -> 22.6 us  [ring_step(): came = lax.ppermute(held, 'dp', ROUTE)]
    dynamic_slice x1 -> x0, local copies, waits for them, and re-layouts: 3.51 us -> none  [body(): lax.dynamic_slice_in_dim(dy, (1 - core) * (D // 2), D // 2, axis=1)]
    ppermute x6 -> x7, waiting for transfers between devices: 0.02 us -> 2.58 us  [swap_cores(): return lax.ppermute(a, 'dp', [(i, i ^ 1) for i in range(2 * N_Z)])]
    pallas_call x1, Pallas kernels: 8.7 us -> 11.2 us  [forward(): pl.pallas_call(forward_kernel, grid=(FF // width,), in_specs=[pl.BlockSpe...]
    ppermute x21, waiting for transfers between devices: 30.3 us -> 28 us  [ring_step(): came = lax.ppermute(held, 'dp', ROUTE)]
    unnamed x32 -> x42, local copies, waits for them, and re-layouts: 10.5 us -> 8.95 us
  transfers between devices with their start and end apart: 30 -> 31, of which waited for: 19 -> 20; matrix products, arithmetic and copies ran while one was open for 6% -> 3% of each run, Pallas kernels for 22% -> 28%
where the time goes in v2:
time: 209 us; the launch traced here: 207 us
  waiting for transfers between devices  72.1 us (34%)
  Pallas kernels  69.7 us (33%)
  starting transfers between devices  47.8 us (23%)
  local copies, waits for them, and re-layouts  11.1 us (5%)
  other arithmetic  5.52 us (3%)
    all_to_all x3, waiting for transfers between devices, exchange_experts(): lax.all_to_all(rows.reshape(N_EXP, CAP, width), 'expert', split_axis=0, c...  41.6 us
    ppermute x21, waiting for transfers between devices, ring_step(): came = lax.ppermute(held, 'dp', ROUTE)  28 us
    all_to_all x3, starting transfers between devices, exchange_experts(): lax.all_to_all(rows.reshape(N_EXP, CAP, width), 'expert', split_axis=0, c...  23.6 us
    ppermute x21, starting transfers between devices, ring_step(): came = lax.ppermute(held, 'dp', ROUTE)  22.6 us
    pallas_call x4, Pallas kernels, outer_sum(): pl.pallas_call(outer_kernel, grid=(n // width,), in_specs=[left, left, pl...  13.8 us
    pallas_call x1, Pallas kernels, forward(): pl.pallas_call(forward_kernel, grid=(FF // width,), in_specs=[pl.BlockSpe...  11.2 us
    unnamed x42, local copies, waits for them, and re-layouts  8.95 us
    pallas_call x1, Pallas kernels, backward(): pl.pallas_call(backward_kernel, grid=(FF // width,), in_specs=[pl.BlockSp...  7.59 us
  transfers between devices with their start and end apart: 31, of which 20 were waited for; matrix products, arithmetic and copies ran while one was open for 3% of the time, Pallas kernels for 28%

profile of v2, /device:TPU:2, one launch (start us, length us, event | category | flops | bytes accessed | tf_op | source)
XLA Modules:
  0.0 207.2 jit_solution(13408163258741845379)
XLA Ops:
  0.6 6.0 %shard_map.111 = bf16[640,3072]{1,0:T(8,128)(2,1)} custom-call(s32[1]{0:T(128)} %bitcast.3.core_ref, s32[4,128]{1,0:T(4,128)} %bitcast.120, bf16[4,128]{1,0:T(4,128)(2,1)} %bitcast.123, bf16[128,2048]{1,0:T(8,128)(2,1)} %x_ref.1, bf16[128,2048]{1,0:T(8,128)(2,1)} %dy_ref.3), custom_call_target="tpu_custom_call" | custom-call | flops 503316480 | bytes 3932160 | tf_op jit(solution)/shard_map/pallas_call | solution.py:80
  6.7 7.5 %all-to-all-start = ((bf16[16,40,3072]{2,1,0:T(8,128)(2,1)}), bf16[16,40,3072]{2,1,0:T(8,128)(2,1)}, u32[]{:S(2)}, u32[]{:S(2)}) async-start(bf16[16,40,3072]{2,1,0:T(8,128)(2,1)} %bitcast.126), calls=%async_computation | async-start | bytes 7864320 | tf_op jit(solution)/shard_map/all_to_all | solution.py:389
  14.1 4.7 %shard_map.112.refs_2_.wd_ref = bf16[2048,768]{1,0:T(8,128)(2,1)} custom-call(s32[1]{0:T(128)} %bitcast.3.core_ref, bf16[1,768,2048]{2,1,0:T(8,128)(2,1)} %w_ref.1), custom_call_target="tpu_custom_call" | custom-call | bytes 6291456 | tf_op jit(solution)/shard_map/pallas_call | solution.py:139
  18.8 6.1 %shard_map.113 = (bf16[768,2048]{1,0:T(8,128)(2,1)}, bf16[768,2048]{1,0:T(8,128)(2,1)}) custom-call(bf16[1,2048,768]{2,1,0:T(8,128)(2,1)} %wg_ref.1, bf16[1,2048,768]{2,1,0:T(8,128)(2,1)} %wu_ref.1), custom_call_target="tpu_custom_call" | custom-call | bytes 12582912 | tf_op jit(solution)/shard_map/pallas_call | solution.py:162
  24.9 2.6 %shard_map.110.refs_0_ = bf16[640,1024]{1,0:T(8,128)(2,1)} custom-call(s32[1]{0:T(128)} %bitcast.3.core_ref, s32[4,128]{1,0:T(4,128)} %bitcast.121, bf16[4,128]{1,0:T(4,128)(2,1)} %bitcast.124, bf16[128,2048]{1,0:T(8,128)(2,1)} %dy_ref.3), custom_call_target="tpu_custom_call" | custom-call | flops 167772160 | bytes 1310720 | tf_op jit(solution)/shard_map/pallas_call | solution.py:114
  27.5 41.6 %all-to-all-done = bf16[16,40,3072]{2,1,0:T(8,128)(2,1)} async-done(((bf16[16,40,3072]{2,1,0:T(8,128)(2,1)}), bf16[16,40,3072]{2,1,0:T(8,128)(2,1)}, u32[]{:S(2)}, u32[]{:S(2)}) %all-to-all-start) | async-done | bytes 3932192 | tf_op jit(solution)/shard_map/all_to_all | solution.py:389
  69.1 6.4 %shard_map.117 = (bf16[1024,640]{1,0:T(8,128)(2,1)}, bf16[1024,640]{1,0:T(8,128)(2,1)}) custom-call(s32[1]{0:T(128)} %bitcast.3.core_ref, bf16[640,3072]{1,0:T(8,128)(2,1)} %bitcast.5.refs_1_.x_ref.dy_ref.a_ref.after_ref.mine_ref.theirs_ref, bf16[640,3072]{1,0:T(8,128)(2,1)} %bitcast.5.refs_1_.x_ref.dy_ref.a_ref.after_ref.mine_ref.theirs_ref), custom_call_target="tpu_custom_call" | custom-call | bytes 5242880 | tf_op jit(solution)/shard_map/pallas_call | solution.py:216
  75.5 8.9 %all-to-all-start.1 = ((bf16[16,40,1024]{2,1,0:T(8,128)(2,1)}), bf16[16,40,1024]{2,1,0:T(8,128)(2,1)S(1)}, u32[]{:S(2)}, u32[]{:S(2)}) async-start(bf16[16,40,1024]{2,1,0:T(8,128)(2,1)} %bitcast.127), calls=%async_computation.1 | async-start | bytes 2621440 | tf_op jit(solution)/shard_map/all_to_all | solution.py:389
  84.4 11.2 %shard_map.115 = (bf16[768,640]{1,0:T(8,128)(2,1)}, f32[640,768]{1,0:T(8,128)}, f32[640,768]{1,0:T(8,128)}, f32[640,768]{1,0:T(8,128)}, f32[640,768]{1,0:T(8,128)}) custom-call(bf16[640,3072]{1,0:T(8,128)(2,1)} %bitcast.5.refs_1_.x_ref.dy_ref.a_ref.after_ref.mine_ref.theirs_ref, ...), custom_call_target="tpu_custom_call" | custom-call | flops 5033164800 | bytes 20000000 | tf_op jit(solution)/shard_map/pallas_call | solution.py:191
  97.5 2.0 collective-permute-done.1.b_ref
  99.5 2.6 %shard_map.116.refs_1_.after_ref = bf16[768,1024]{1,0:T(8,128)(2,1)S(1)} custom-call(bf16[768,640]{1,0:T(8,128)(2,1)S(1)} %copy-done.9, bf16[768,640]{1,0:T(8,128)(2,1)S(1)} %collective-permute-done.bt_ref, bf16[640,3072]{1,0:T(8,128)(2,1)} %bitcast.5.refs_1_.x_ref.dy_ref.a_ref.after_ref.mine_ref.theirs_ref, ...), custom_call_target="tpu_custom_call" | custom-call | flops 1006632960 | bytes 4063232 | tf_op jit(solution)/shard_map/pallas_call | solution.py:328
  105.9 7.6 %shard_map.119 = (bf16[640,768]{1,0:T(8,128)(2,1)}, bf16[640,768]{1,0:T(8,128)(2,1)}, bf16[640,128]{1,0:T(8,128)(2,1)}) custom-call(s32[1]{0:T(128)} %bitcast.2.me_ref, bf16[640,1024]{1,0:T(8,128)(2,1)} %shard_map.118.dy_ref.a_ref, bf16[2048,768]{1,0:T(8,128)(2,1)} %shard_map.112.refs_2_.wd_ref, f32[640,768]{1,0:T(8,128)} %get-tuple-element.22.h_ref, ...), custom_call_target="tpu_custom_call" | custom-call | flops 1006632960 | bytes 12000000 | tf_op jit(solution)/shard_map/pallas_call | solution.py:262
  116.5 2.8 %shard_map.120.after_ref = bf16[768,1024]{1,0:T(8,128)(2,1)S(1)} custom-call(bf16[768,640]{1,0:T(8,128)(2,1)S(1)} %copy-done.10, bf16[768,640]{1,0:T(8,128)(2,1)S(1)} %copy-done.12, bf16[640,1024]{1,0:T(8,128)(2,1)S(1)} %copy-done.3, bf16[640,1024]{1,0:T(8,128)(2,1)} %collective-permute-done.3.b_ref, ...), custom_call_target="tpu_custom_call", output_to_operand_aliasing={{}: (4, {})} | custom-call | flops 1006632960 | bytes 4063232 | tf_op jit(solution)/shard_map/pallas_call | solution.py:328
  119.4 2.2 %collective-permute-start.20 = (bf16[96,1024]{1,0:T(8,128)(2,1)S(1)}, bf16[96,1024]{1,0:T(8,128)(2,1)S(1)}, u32[]{:S(2)}, u32[]{:S(2)}) collective-permute-start(bf16[96,1024]{1,0:T(8,128)(2,1)S(1)} %dynamic-slice_bitcast_fusion), channel_id=1, source_target_pairs={{0,32},{32,64},{64,96},{96,128},{128,160},{160,192},{192,224},{224... | collective-permute-start | bytes 589832 | tf_op jit(solution)/shard_map/ppermute | solution.py:427
  123.5 6.8 %shard_map.121.after_ref.refs_0_ = bf16[640,2176]{1,0:T(8,128)(2,1)} custom-call(bf16[640,768]{1,0:T(8,128)(2,1)S(1)} %copy-done.14, bf16[640,768]{1,0:T(8,128)(2,1)S(1)} %copy-done.15, bf16[768,2048]{1,0:T(8,128)(2,1)S(1)} %copy-done.13, bf16[768,2048]{1,0:T(8,128)(2,1)S(1)} %copy-done.19, bf16[640,128]{1,0:T(8,128)(2,1)S(1)} %copy-done.20, ...), custom_call_target="tpu_custom_call" | custom-call | flops 4026531840 | bytes 12000000 | tf_op jit(solution)/shard_map/pallas_call | solution.py:301
  130.3 4.1 %shard_map.123.refs_2_ = bf16[1024,768]{1,0:T(8,128)(2,1)S(1)} custom-call(bf16[1024,640]{1,0:T(8,128)(2,1)S(1)} %copy-done.8, bf16[1024,640]{1,0:T(8,128)(2,1)S(1)} %copy-done.7, bf16[640,768]{1,0:T(8,128)(2,1)S(1)} %copy-done.15, bf16[640,768]{1,0:T(8,128)(2,1)} %collective-permute-done.5.b_ref, bf16[640,2176]{1,0:T(8,128)(2,1)} %shard_map.121.after_ref.refs_0_), custom_call_target="tpu_custom_call" | custom-call | flops 2013265920 | bytes 6160384 | tf_op jit(solution)/shard_map/pallas_call | solution.py:328
  134.4 4.3 %shard_map.122.refs_1_ = bf16[1024,768]{1,0:T(8,128)(2,1)S(1)} custom-call(bf16[1024,640]{1,0:T(8,128)(2,1)S(1)} %copy-done.8, bf16[1024,640]{1,0:T(8,128)(2,1)S(1)} %copy-done.7, bf16[640,768]{1,0:T(8,128)(2,1)S(1)} %copy-done.14, bf16[640,768]{1,0:T(8,128)(2,1)} %collective-permute-done.4.b_ref, bf16[640,2176]{1,0:T(8,128)(2,1)} %shard_map.121.after_ref.refs_0_), custom_call_target="tpu_custom_call" | custom-call | flops 2013265920 | bytes 6160384 | tf_op jit(solution)/shard_map/pallas_call | solution.py:328
  138.7 7.2 %all-to-all-start.2 = ((bf16[16,40,2176]{2,1,0:T(8,128)(2,1)}), bf16[16,40,2176]{2,1,0:T(8,128)(2,1)}, u32[]{:S(2)}, u32[]{:S(2)}) async-start(bf16[16,40,2176]{2,1,0:T(8,128)(2,1)} %bitcast.8), calls=%async_computation.2 | async-start | bytes 5570560 | tf_op jit(solution)/shard_map/all_to_all | solution.py:389
  150.9 3.3 %collective-permute-start.21 = (bf16[96,1024]{1,0:T(8,128)(2,1)S(1)}, bf16[96,1024]{1,0:T(8,128)(2,1)S(1)}, u32[]{:S(2)}, u32[]{:S(2)}) collective-permute-start(bf16[96,1024]{1,0:T(8,128)(2,1)S(1)} %shard_map.126), channel_id=1, source_target_pairs={{0,32},{32,64},{64,96},{96,128},{128,160},{160,192},{192,224},{224... | collective-permute-start | bytes 589832 | tf_op jit(solution)/shard_map/ppermute | solution.py:427
  166.6 2.0 collective-permute-done.15
  185.5 4.1 %collective-permute-done.18 = bf16[128,768]{1,0:T(8,128)(2,1)S(1)} collective-permute-done((bf16[128,768]{1,0:T(8,128)(2,1)S(1)}, bf16[128,768]{1,0:T(8,128)(2,1)S(1)}, u32[]{:S(2)}, u32[]{:S(2)}) %collective-permute-start.18) | collective-permute-done | bytes 196640 | tf_op jit(solution)/shard_map/ppermute | solution.py:427
  192.6 4.5 %shard_map.125 = (bf16[128,2048]{1,0:T(8,128)(2,1)}, bf16[4,128]{1,0:T(4,128)(2,1)}) custom-call(s32[4,128]{1,0:T(4,128)S(1)} %bitcast.122, bf16[4,128]{1,0:T(4,128)(2,1)S(1)} %bitcast.125, bf16[640,2176]{1,0:T(8,128)(2,1)} %bitcast.9.rows_ref.extra_ref, bf16[640,2176]{1,0:T(8,128)(2,1)} %bitcast.9.rows_ref.extra_ref), custom_call_target="tpu_custom_call" | custom-call | flops 335544320 | bytes 2621440 | tf_op jit(solution)/shard_map/pallas_call | solution.py:367
  198.2 2.2 %collective-permute-start.26 = (bf16[96,1024]{1,0:T(8,128)(2,1)S(1)}, bf16[96,1024]{1,0:T(8,128)(2,1)S(1)}, u32[]{:S(2)}, u32[]{:S(2)}) collective-permute-start(bf16[96,1024]{1,0:T(8,128)(2,1)S(1)} %shard_map.127), channel_id=1, source_target_pairs={{0,32},{32,64},{64,96},{96,128},{128,160},{160,192},{192,224},{224... | collective-permute-start | bytes 589832 | tf_op jit(solution)/shard_map/ppermute | solution.py:427
  202.1 2.9 %collective-permute-done.26 = bf16[96,1024]{1,0:T(8,128)(2,1)S(1)} collective-permute-done((bf16[96,1024]{1,0:T(8,128)(2,1)S(1)}, bf16[96,1024]{1,0:T(8,128)(2,1)S(1)}, u32[]{:S(2)}, u32[]{:S(2)}) %collective-permute-start.26) | collective-permute-done | bytes 196640 | tf_op jit(solution)/shard_map/ppermute | solution.py:427
  (126 shorter events, 52.6 us)
Async XLA Ops:
  6.7 62.5 %all-to-all-start = ((bf16[16,40,3072]{2,1,0:T(8,128)(2,1)}), bf16[16,40,3072]{2,1,0:T(8,128)(2,1)}, u32[]{:S(2)}, u32[]{:S(2)}) async-start(bf16[16,40,3072]{2,1,0:T(8,128)(2,1)} %bitcast.126), calls=%async_computation | async-start | bytes 7864320 | tf_op jit(solution)/shard_map/all_to_all | solution.py:389
  75.5 28.8 %all-to-all-start.1 = ((bf16[16,40,1024]{2,1,0:T(8,128)(2,1)}), bf16[16,40,1024]{2,1,0:T(8,128)(2,1)S(1)}, u32[]{:S(2)}, u32[]{:S(2)}) async-start(bf16[16,40,1024]{2,1,0:T(8,128)(2,1)} %bitcast.127), calls=%async_computation.1 | async-start | bytes 2621440 | tf_op jit(solution)/shard_map/all_to_all | solution.py:389
  84.4 19.9 %collective-permute-start.2 = (bf16[1024,640]{1,0:T(8,128)(2,1)}, bf16[1024,640]{1,0:T(8,128)(2,1)S(1)}, u32[]{:S(2)}, u32[]{:S(2)}) collective-permute-start(bf16[1024,640]{1,0:T(8,128)(2,1)} %get-tuple-element.21), channel_id=1, source_target_pairs={{0,16},{16,0},{32,48},{48,32},{64,80},{80,64},{96,112},{112,96},{1... | collective-permute-start | bytes 3932168 | tf_op jit(solution)/shard_map/ppermute | solution.py:412
  105.8 8.3 %collective-permute-start.3 = (bf16[640,1024]{1,0:T(8,128)(2,1)}, bf16[640,1024]{1,0:T(8,128)(2,1)}, u32[]{:S(2)}, u32[]{:S(2)}) collective-permute-start(bf16[640,1024]{1,0:T(8,128)(2,1)} %shard_map.118.dy_ref.a_ref), channel_id=1, source_target_pairs={{0,16},{16,0},{32,48},{48,32},{64,80},{80,64},{96,112},{112,96},{1... | collective-permute-start | bytes 3932168 | tf_op jit(solution)/shard_map/ppermute | solution.py:412
  113.5 16.7 %collective-permute-start.5 = (bf16[640,768]{1,0:T(8,128)(2,1)}, bf16[640,768]{1,0:T(8,128)(2,1)}, u32[]{:S(2)}, u32[]{:S(2)}) collective-permute-start(bf16[640,768]{1,0:T(8,128)(2,1)} %get-tuple-element.27.du_ref.a_ref), channel_id=1, source_target_pairs={{0,16},{16,0},{32,48},{48,32},{64,80},{80,64},{96,112},{112,96},{1... | collective-permute-start | bytes 2949128 | tf_op jit(solution)/shard_map/ppermute | solution.py:412
  113.9 20.5 %collective-permute-start.4 = (bf16[640,768]{1,0:T(8,128)(2,1)}, bf16[640,768]{1,0:T(8,128)(2,1)}, u32[]{:S(2)}, u32[]{:S(2)}) collective-permute-start(bf16[640,768]{1,0:T(8,128)(2,1)} %get-tuple-element.26.dg_ref.a_ref), channel_id=1, source_target_pairs={{0,16},{16,0},{32,48},{48,32},{64,80},{80,64},{96,112},{112,96},{1... | collective-permute-start | bytes 2949128 | tf_op jit(solution)/shard_map/ppermute | solution.py:412
  119.4 31.5 %collective-permute-start.20 = (bf16[96,1024]{1,0:T(8,128)(2,1)S(1)}, bf16[96,1024]{1,0:T(8,128)(2,1)S(1)}, u32[]{:S(2)}, u32[]{:S(2)}) collective-permute-start(bf16[96,1024]{1,0:T(8,128)(2,1)S(1)} %dynamic-slice_bitcast_fusion), channel_id=1, source_target_pairs={{0,32},{32,64},{64,96},{96,128},{128,160},{160,192},{192,224},{224... | collective-permute-start | bytes 589832 | tf_op jit(solution)/shard_map/ppermute | solution.py:427
  138.7 53.9 %all-to-all-start.2 = ((bf16[16,40,2176]{2,1,0:T(8,128)(2,1)}), bf16[16,40,2176]{2,1,0:T(8,128)(2,1)}, u32[]{:S(2)}, u32[]{:S(2)}) async-start(bf16[16,40,2176]{2,1,0:T(8,128)(2,1)} %bitcast.8), calls=%async_computation.2 | async-start | bytes 5570560 | tf_op jit(solution)/shard_map/all_to_all | solution.py:389
  146.9 7.7 %collective-permute-start.13 = (bf16[128,768]{1,0:T(8,128)(2,1)S(1)}, bf16[128,768]{1,0:T(8,128)(2,1)S(1)}, u32[]{:S(2)}, u32[]{:S(2)}) collective-permute-start(bf16[128,768]{1,0:T(8,128)(2,1)S(1)} %dynamic-slice_bitcast_fusion.1), channel_id=1, source_target_pairs={{0,32},{32,64},{64,96},{96,128},{128,160},{160,192},{192,224},{224... | collective-permute-start | bytes 589832 | tf_op jit(solution)/shard_map/ppermute | solution.py:427
  148.9 7.8 %collective-permute-start.6 = (bf16[128,768]{1,0:T(8,128)(2,1)S(1)}, bf16[128,768]{1,0:T(8,128)(2,1)S(1)}, u32[]{:S(2)}, u32[]{:S(2)}) collective-permute-start(bf16[128,768]{1,0:T(8,128)(2,1)S(1)} %dynamic-slice_bitcast_fusion.2), channel_id=1, source_target_pairs={{0,32},{32,64},{64,96},{96,128},{128,160},{160,192},{192,224},{224... | collective-permute-start | bytes 589832 | tf_op jit(solution)/shard_map/ppermute | solution.py:427
  150.9 7.9 %collective-permute-start.21 = (bf16[96,1024]{1,0:T(8,128)(2,1)S(1)}, bf16[96,1024]{1,0:T(8,128)(2,1)S(1)}, u32[]{:S(2)}, u32[]{:S(2)}) collective-permute-start(bf16[96,1024]{1,0:T(8,128)(2,1)S(1)} %shard_map.126), channel_id=1, source_target_pairs={{0,32},{32,64},{64,96},{96,128},{128,160},{160,192},{192,224},{224... | collective-permute-start | bytes 589832 | tf_op jit(solution)/shard_map/ppermute | solution.py:427
  154.7 7.0 %collective-permute-start.14 = (bf16[128,768]{1,0:T(8,128)(2,1)S(1)}, bf16[128,768]{1,0:T(8,128)(2,1)S(1)}, u32[]{:S(2)}, u32[]{:S(2)}) collective-permute-start(bf16[128,768]{1,0:T(8,128)(2,1)S(1)} %fusion.13), channel_id=1, source_target_pairs={{0,32},{32,64},{64,96},{96,128},{128,160},{160,192},{192,224},{224... | collective-permute-start | bytes 589832 | tf_op jit(solution)/shard_map/ppermute | solution.py:427
  156.8 7.0 %collective-permute-start.7 = (bf16[128,768]{1,0:T(8,128)(2,1)S(1)}, bf16[128,768]{1,0:T(8,128)(2,1)S(1)}, u32[]{:S(2)}, u32[]{:S(2)}) collective-permute-start(bf16[128,768]{1,0:T(8,128)(2,1)S(1)} %fusion.20), channel_id=1, source_target_pairs={{0,32},{32,64},{64,96},{96,128},{128,160},{160,192},{192,224},{224... | collective-permute-start | bytes 589832 | tf_op jit(solution)/shard_map/ppermute | solution.py:427
  158.9 7.0 %collective-permute-start.22 = (bf16[96,1024]{1,0:T(8,128)(2,1)S(1)}, bf16[96,1024]{1,0:T(8,128)(2,1)S(1)}, u32[]{:S(2)}, u32[]{:S(2)}) collective-permute-start(bf16[96,1024]{1,0:T(8,128)(2,1)S(1)} %fusion.5), channel_id=1, source_target_pairs={{0,32},{32,64},{64,96},{96,128},{128,160},{160,192},{192,224},{224... | collective-permute-start | bytes 589832 | tf_op jit(solution)/shard_map/ppermute | solution.py:427
  161.7 7.0 %collective-permute-start.15 = (bf16[128,768]{1,0:T(8,128)(2,1)S(1)}, bf16[128,768]{1,0:T(8,128)(2,1)S(1)}, u32[]{:S(2)}, u32[]{:S(2)}) collective-permute-start(bf16[128,768]{1,0:T(8,128)(2,1)S(1)} %fusion.12), channel_id=1, source_target_pairs={{0,32},{32,64},{64,96},{96,128},{128,160},{160,192},{192,224},{224... | collective-permute-start | bytes 589832 | tf_op jit(solution)/shard_map/ppermute | solution.py:427
  163.8 7.0 %collective-permute-start.8 = (bf16[128,768]{1,0:T(8,128)(2,1)S(1)}, bf16[128,768]{1,0:T(8,128)(2,1)S(1)}, u32[]{:S(2)}, u32[]{:S(2)}) collective-permute-start(bf16[128,768]{1,0:T(8,128)(2,1)S(1)} %fusion.19), channel_id=1, source_target_pairs={{0,32},{32,64},{64,96},{96,128},{128,160},{160,192},{192,224},{224... | collective-permute-start | bytes 589832 | tf_op jit(solution)/shard_map/ppermute | solution.py:427
  165.9 7.0 %collective-permute-start.23 = (bf16[96,1024]{1,0:T(8,128)(2,1)S(1)}, bf16[96,1024]{1,0:T(8,128)(2,1)S(1)}, u32[]{:S(2)}, u32[]{:S(2)}) collective-permute-start(bf16[96,1024]{1,0:T(8,128)(2,1)S(1)} %fusion.4), channel_id=1, source_target_pairs={{0,32},{32,64},{64,96},{96,128},{128,160},{160,192},{192,224},{224... | collective-permute-start | bytes 589832 | tf_op jit(solution)/shard_map/ppermute | solution.py:427
  168.7 7.0 %collective-permute-start.16 = (bf16[128,768]{1,0:T(8,128)(2,1)S(1)}, bf16[128,768]{1,0:T(8,128)(2,1)S(1)}, u32[]{:S(2)}, u32[]{:S(2)}) collective-permute-start(bf16[128,768]{1,0:T(8,128)(2,1)S(1)} %fusion.11), channel_id=1, source_target_pairs={{0,32},{32,64},{64,96},{96,128},{128,160},{160,192},{192,224},{224... | collective-permute-start | bytes 589832 | tf_op jit(solution)/shard_map/ppermute | solution.py:427
  170.8 7.0 %collective-permute-start.9 = (bf16[128,768]{1,0:T(8,128)(2,1)S(1)}, bf16[128,768]{1,0:T(8,128)(2,1)S(1)}, u32[]{:S(2)}, u32[]{:S(2)}) collective-permute-start(bf16[128,768]{1,0:T(8,128)(2,1)S(1)} %fusion.18), channel_id=1, source_target_pairs={{0,32},{32,64},{64,96},{96,128},{128,160},{160,192},{192,224},{224... | collective-permute-start | bytes 589832 | tf_op jit(solution)/shard_map/ppermute | solution.py:427
  172.9 7.2 %collective-permute-start.24 = (bf16[96,1024]{1,0:T(8,128)(2,1)S(1)}, bf16[96,1024]{1,0:T(8,128)(2,1)S(1)}, u32[]{:S(2)}, u32[]{:S(2)}) collective-permute-start(bf16[96,1024]{1,0:T(8,128)(2,1)S(1)} %fusion.3), channel_id=1, source_target_pairs={{0,32},{32,64},{64,96},{96,128},{128,160},{160,192},{192,224},{224... | collective-permute-start | bytes 589832 | tf_op jit(solution)/shard_map/ppermute | solution.py:427
  175.7 7.0 %collective-permute-start.17 = (bf16[128,768]{1,0:T(8,128)(2,1)S(1)}, bf16[128,768]{1,0:T(8,128)(2,1)S(1)}, u32[]{:S(2)}, u32[]{:S(2)}) collective-permute-start(bf16[128,768]{1,0:T(8,128)(2,1)S(1)} %fusion.10), channel_id=1, source_target_pairs={{0,32},{32,64},{64,96},{96,128},{128,160},{160,192},{192,224},{224... | collective-permute-start | bytes 589832 | tf_op jit(solution)/shard_map/ppermute | solution.py:427
  180.2 12.4 %collective-permute-start.25 = (bf16[96,1024]{1,0:T(8,128)(2,1)S(1)}, bf16[96,1024]{1,0:T(8,128)(2,1)S(1)}, u32[]{:S(2)}, u32[]{:S(2)}) collective-permute-start(bf16[96,1024]{1,0:T(8,128)(2,1)S(1)} %fusion.2), channel_id=1, source_target_pairs={{0,32},{32,64},{64,96},{96,128},{128,160},{160,192},{192,224},{224... | collective-permute-start | bytes 589832 | tf_op jit(solution)/shard_map/ppermute | solution.py:427
  190.4 10.0 %collective-permute-start.19 = (bf16[128,768]{1,0:T(8,128)(2,1)}, bf16[128,768]{1,0:T(8,128)(2,1)}, u32[]{:S(2)}, u32[]{:S(2)}) collective-permute-start(bf16[128,768]{1,0:T(8,128)(2,1)} %fusion.8), channel_id=1, source_target_pairs={{0,32},{32,64},{64,96},{96,128},{128,160},{160,192},{192,224},{224... | collective-permute-start | bytes 589832 | tf_op jit(solution)/shard_map/ppermute | solution.py:427
  192.5 12.7 %collective-permute-start.12 = (bf16[128,768]{1,0:T(8,128)(2,1)}, bf16[128,768]{1,0:T(8,128)(2,1)S(1)}, u32[]{:S(2)}, u32[]{:S(2)}) collective-permute-start(bf16[128,768]{1,0:T(8,128)(2,1)} %fusion.15), channel_id=1, source_target_pairs={{0,32},{32,64},{64,96},{96,128},{128,160},{160,192},{192,224},{224... | collective-permute-start | bytes 589832 | tf_op jit(solution)/shard_map/ppermute | solution.py:427
  (28 other events, 132.3 us)
